TPU v7x, 1024 devices: a whole 8x8x8 slice. The times are simulated.
1024 devices in a mesh: cols: 64 (over x, z), fld: 16 (over y, core).
Axes of the slice: x: 8, y: 8, z: 8, core: 2. Of those that a mesh axis runs over, the one named last changes fastest.
Arguments:
- atm_state: bfloat16 [16, 8, 229376], P('fld', None, 'cols'), may hold values from -4 to 4
- owners: int32 [1792, 4], P('cols'), may hold values from 0 to 63, all different within a row; in each aligned block of 28 rows (0 to 27, 28 to 55, ...) at most 3 rows name the same one
- ocean_tile: int32 [1792, 4], P('cols'), may hold values from 0 to 6
- centroid_offset: float32 [1792, 4, 128], P('cols'), may hold values from -0.5 to 0.5
- remap_weight: bfloat16 [1792, 4, 128, 128], P('cols'), may hold values from 0 to 1, as said below
- ocean_state: float32 [4, 57344], P(None, 'cols'), may hold values from -4 to 4
Outputs:
- sample_fluxes: float32 [16, 4, 57344], P('fld', None, 'cols')
- ocean_next: float32 [4, 57344], P(None, 'cols')
- atm_surface: float32 [4, 229376], P(None, 'cols')
Inputs may be any that keep to these rules, and one draw needn't show every extreme that they name: In each device's aligned block of 28 rows no owner appears more than 3 times, and the 4 owners of a row differ. `remap_weight`: entries are nonnegative.
All inputs are finite; a program needn't handle non-finite values.
Results may differ from a plain program's by a relative error of at most 0.00078.
Values may be sent and summed in bfloat16 or wider, within the bound.
A program may use at most 32 MiB of HBM per device.

v0:
```python
import jax
import jax.numpy as jnp
from jax import lax
from jax.sharding import PartitionSpec as P

TILE = 128


def padded_2(block, sides, width):
    for axis, dim in sides:
        count = lax.axis_size(axis)
        forward = [(i, i + 1) for i in range(count - 1)]
        forward.append((count - 1, 0))
        backward = [(target, source) for source, target in forward]
        low = lax.ppermute(
            lax.slice_in_dim(block, block.shape[dim] - width, None, axis=dim), axis, forward
        )
        high = lax.ppermute(lax.slice_in_dim(block, 0, width, axis=dim), axis, backward)
        block = jnp.concatenate([low, block, high], axis=dim)
    return block


def surface_fluxes(forcing, ocean_now, insolation):
    slip_u = forcing[0] - ocean_now[1]
    slip_v = forcing[1] - ocean_now[2]
    wind_speed = jnp.sqrt(slip_u * slip_u + slip_v * slip_v + 0.25)
    saturation = 0.9 * jnp.exp(0.07 * ocean_now[0] - 0.1 * forcing[4])
    sensible = 0.4 * wind_speed * (ocean_now[0] - forcing[2])
    latent = 0.4 * wind_speed * (saturation - forcing[3])
    net_heat = (
        insolation * jax.nn.softplus(forcing[5])
        + 0.3 * forcing[6]
        - 0.1 * ocean_now[0]
        - sensible
        - latent
    )
    freshwater = jax.nn.softplus(forcing[7]) - latent
    return jnp.stack([0.5 * wind_speed * slip_u, 0.5 * wind_speed * slip_v, net_heat, freshwater])


def shards(atm_state, owners, ocean_tile, centroid_offset, remap_weight, ocean_state):
    col_count = lax.axis_size("cols")
    fld_count = lax.axis_size("fld")
    samples_here, fields, cells = atm_state.shape
    tile_len = TILE
    tiles = cells // tile_len
    reach = owners.shape[1]
    otiles = ocean_state.shape[1] // tile_len
    row_count = samples_here * fields
    entries = tiles * reach
    padded = padded_2(atm_state, (("cols", 2),), 1)
    widened = padded.astype(jnp.float32)
    values = widened[:, :, 1:-1]
    slope = 0.5 * (widened[:, :, 2:] - widened[:, :, :-2])
    value_tiles = values.reshape(row_count, tiles, tile_len).transpose(1, 0, 2)
    slope_tiles = slope.reshape(row_count, tiles, tile_len).transpose(1, 0, 2)
    rebuilt = (value_tiles[:, None] + centroid_offset[:, :, None, :] * slope_tiles[:, None]).astype(
        jnp.bfloat16
    )
    partials = jnp.einsum(
        "tkra,tkoa->tkro", rebuilt, remap_weight, preferred_element_type=jnp.float32
    )
    partials = partials.reshape(entries, row_count, tile_len)
    intersection_area = jnp.sum(remap_weight, axis=3, dtype=jnp.float32).reshape(entries, tile_len)
    owner_of = owners.reshape(entries)
    tile_index = ocean_tile.reshape(entries)
    tile_key = owner_of * otiles + tile_index
    selector = (tile_key[:, None] == jnp.arange(col_count * otiles)[None, :]).astype(jnp.float32)
    outgoing = jnp.einsum("eq,erc->qrc", selector, partials, precision=lax.Precision.HIGHEST)
    outgoing_area = jnp.einsum(
        "eq,ec->qc", selector, intersection_area, precision=lax.Precision.HIGHEST
    )
    incoming, incoming_area = (
        lax.all_to_all(
            outgoing.reshape(col_count, otiles, row_count, tile_len),
            "cols",
            split_axis=0,
            concat_axis=0,
            tiled=True,
        ),
        lax.all_to_all(
            outgoing_area.reshape(col_count, otiles, tile_len),
            "cols",
            split_axis=0,
            concat_axis=0,
            tiled=True,
        ),
    )
    gathered_sums = jnp.sum(incoming, axis=0)
    coverage = jnp.sum(incoming_area, axis=0)
    forcing = gathered_sums / jnp.maximum(coverage, 1.0)[:, None, :]
    forcing = (
        forcing.reshape(otiles, samples_here, fields, tile_len)
        .transpose(1, 2, 0, 3)
        .reshape(samples_here, fields, otiles * tile_len)
    )
    first_sample = lax.axis_index("fld") * samples_here
    insolation = 0.5 + 1.5 * (first_sample + jnp.arange(samples_here)).astype(jnp.float32) / (
        samples_here * fld_count - 1
    )
    sample_fluxes = jax.vmap(surface_fluxes, in_axes=(0, None, 0))(forcing, ocean_state, insolation)
    flux_total = lax.psum(jnp.sum(sample_fluxes, axis=0), "fld")
    mean_flux = flux_total / (samples_here * fld_count)
    ocean_next = ocean_state + 0.5 * jnp.stack(
        [mean_flux[2], mean_flux[0], mean_flux[1], -mean_flux[3]]
    )
    all_states = lax.all_gather(ocean_next, "cols", axis=1, tiled=True)
    entry_state = jnp.take(
        all_states.reshape(4, col_count * otiles, tile_len), tile_key, axis=1
    ).transpose(1, 0, 2)
    remapped = jnp.einsum(
        "tkso,tkoa->tksa",
        entry_state.reshape(tiles, reach, 4, tile_len),
        remap_weight.astype(jnp.float32),
        precision=lax.Precision.HIGHEST,
    )
    remapped = jnp.sum(remapped, axis=1)
    column_area = jnp.sum(jnp.sum(remap_weight, axis=2, dtype=jnp.float32), axis=1)
    atm_surface = (remapped / column_area[:, None, :]).transpose(1, 0, 2).reshape(4, cells)
    return (sample_fluxes, ocean_next, atm_surface)


def solution(mesh):
    return jax.shard_map(
        shards,
        mesh=mesh,
        in_specs=(
            P("fld", None, "cols"),
            P("cols", None),
            P("cols", None),
            P("cols", None, None),
            P("cols", None, None, None),
            P(None, "cols"),
        ),
        out_specs=(P("fld", None, "cols"), P(None, "cols"), P(None, "cols")),
        check_vma=False,
    )
```

profile of v0, /device:TPU:4, one launch (start us, length us, event | category | flops | bytes accessed | tf_op | source)
XLA Modules:
  0.0 203.9 jit_solution(8714417631526644305)
XLA Ops:
  0.6 0.0 copy-start
  0.6 0.0 copy-start.1
  0.6 0.8 fusion.37
  1.5 5.2 %collective-permute-start = (bf16[1,8,1]{2,1,0:T(8,128)(2,1)S(1)}, bf16[1,8,1]{2,1,0:T(8,128)(2,1)S(1)}, u32[]{:S(2)}, u32[]{:S(2)}) collective-permute-start(bf16[1,8,1]{2,1,0:T(8,128)(2,1)S(1)} %get-tuple-element.12), channel_id=1, source_target_pairs={{0,16},{16,32},{32,48},{48,64},{64,80},{80,96},{96,112},{112,128},... | collective-permute-start | bytes 56 | tf_op jit(solution)/shard_map/ppermute | solution.py:15
  6.6 14.0 %collective-permute-start.1 = (bf16[1,8,1]{2,1,0:T(8,128)(2,1)S(1)}, bf16[1,8,1]{2,1,0:T(8,128)(2,1)S(1)}, u32[]{:S(2)}, u32[]{:S(2)}) collective-permute-start(bf16[1,8,1]{2,1,0:T(8,128)(2,1)S(1)} %get-tuple-element.11), channel_id=1, source_target_pairs={{16,0},{32,16},{48,32},{64,48},{80,64},{96,80},{112,96},{128,112},... | collective-permute-start | bytes 56 | tf_op jit(solution)/shard_map/ppermute | solution.py:18
  20.7 0.7 multiply_add_fusion.1
  21.4 0.1 copy.16
  21.5 0.1 add.108
  21.6 3.5 %convert_reduce_fusion = (f32[28,128]{1,0:T(8,128)S(1)}, f32[28,4,128]{2,1,0:T(4,128)S(1)}) fusion(bf16[28,4,128,128]{3,2,1,0:T(8,128)(2,1)} %param.10), kind=kLoop, calls=%fused_computation.1 | loop fusion | flops 5487104 | bytes 3741696 | tf_op jit(solution)/shard_map/reduce_sum | solution.py:118
  25.1 0.3 fusion.5
  25.4 0.8 copy.19
  26.3 9.3 %all-to-all-start.1 = ((f32[64,7,128]{2,1,0:T(8,128)}), f32[64,7,128]{2,1,0:T(8,128)S(1)}, u32[]{:S(2)}, u32[]{:S(2)}) async-start(f32[64,7,128]{2,1,0:T(8,128)} %copy.19), calls=%async_computation.1 | async-start | bytes 524288 | tf_op jit(solution)/shard_map/all_to_all | solution.py:81
  35.6 0.0 collective-permute-done
  35.6 0.0 collective-permute-done.1
  35.6 0.0 copy-done
  35.6 0.1 concatenate.11
  35.7 0.1 slice_bitcast_fusion
  35.9 0.0 copy-done.1
  35.9 4.0 %fusion.7 = f32[28,4,8,128]{3,2,1,0:T(8,128)S(1)} fusion(bf16[28,4,128,128]{3,2,1,0:T(8,128)(2,1)} %param.10, f32[28,8,128]{2,1,0:T(8,128)S(1)} %get-tuple-element.10, f32[28,4,128]{2,1,0:T(4,128)S(1)} %copy-done.1, f32[28,8,128]{2,1,0:T(8,128)S(1)} %get-tuple-element.9), kind=kOutput, calls=%fused_computation.13 | convolution fusion | flops 29704192 | bytes 4415488 | tf_op jit(solution)/shard_map/tkra,tkoa->tkro/dot_general | solution.py:60
  39.9 1.0 fusion.2
  40.9 2.3 %copy.18 = f32[64,7,8,128]{3,2,1,0:T(8,128)} copy(f32[64,7,8,128]{3,0,2,1:T(8,128)S(1)} %fusion.2) | data formatting | bytes 3670016 | tf_op jit(solution)/shard_map/eq,erc->qrc/dot_general | solution.py:69
  43.2 0.0 copy-start.3
  43.2 5.7 %all-to-all-done.1 = f32[64,7,128]{2,1,0:T(8,128)S(1)} async-done(((f32[64,7,128]{2,1,0:T(8,128)}), f32[64,7,128]{2,1,0:T(8,128)S(1)}, u32[]{:S(2)}, u32[]{:S(2)}) %all-to-all-start.1) | async-done | bytes 229408 | tf_op jit(solution)/shard_map/all_to_all | solution.py:81
  48.9 7.1 %all-to-all-start = ((f32[64,7,8,128]{3,2,1,0:T(8,128)}), f32[64,7,8,128]{3,2,1,0:T(8,128)S(1)}, u32[]{:S(2)}, u32[]{:S(2)}) async-start(f32[64,7,8,128]{3,2,1,0:T(8,128)} %copy.18), calls=%async_computation | async-start | bytes 3670016 | tf_op jit(solution)/shard_map/all_to_all | solution.py:74
  56.0 0.1 add.121
  56.2 0.1 reduce_sum.48
  56.3 45.3 %all-to-all-done = f32[64,7,8,128]{3,2,1,0:T(8,128)S(1)} async-done(((f32[64,7,8,128]{3,2,1,0:T(8,128)}), f32[64,7,8,128]{3,2,1,0:T(8,128)S(1)}, u32[]{:S(2)}, u32[]{:S(2)}) %all-to-all-start) | async-done | bytes 1835040 | tf_op jit(solution)/shard_map/all_to_all | solution.py:74
  101.5 0.1 reduce_sum.42
  101.7 0.0 copy-done.3
  101.7 0.1 subtract_bitcast_fusion
  101.8 0.6 fusion.33
  102.4 47.0 %psum.7 = f32[4,896]{1,0:T(4,128)S(1)} all-reduce(f32[4,896]{1,0:T(4,128)S(1)} %get-tuple-element.16), channel_id=1, replica_groups=mesh['cols'=64,'fld'=16] {'fld'}, use_global_device_ids=true, to_apply=%region_3.4 | all-reduce | flops 3584 | bytes 28672 | tf_op jit(solution)/shard_map/psum | solution.py:102
  149.5 0.0 copy-start.2
  149.5 49.2 %all_gather.3 = f32[4,57344]{1,0:T(4,128)S(1)} all-gather(f32[4,896]{1,0:T(4,128)S(1)} %fusion.18), channel_id=1, replica_groups=mesh['cols'=64,'fld'=16] {'cols'}, dimensions={1}, use_global_device_ids=true | all-gather | bytes 931840 | tf_op jit(solution)/shard_map/all_gather | solution.py:107
  198.7 0.7 gather_fusion
  199.5 0.2 broadcast_select_fusion
  199.7 4.2 %fusion.1 = f32[4,3584]{1,0:T(4,128)} fusion(f32[28,4,4,128]{3,2,1,0:T(4,128)S(1)} %bitcast.123, bf16[28,4,128,128]{3,2,1,0:T(8,128)(2,1)} %param.10, f32[28,128]{1,0:T(8,128)S(1)} %get-tuple-element.3), kind=kOutput, calls=%fused_computation.5 | convolution fusion | flops 88094720 | bytes 3971072 | tf_op jit(solution)/shard_map/tkso,tkoa->tksa/dot_general | solution.py:111
  203.9 0.0 copy-done.2
  (13 shorter events, 0.1 us)
Async XLA Ops:
  0.6 35.0 %copy-start = (bf16[1,8,3584]{2,1,0:T(8,128)(2,1)S(1)}, bf16[1,8,3584]{2,1,0:T(8,128)(2,1)}, u32[]{:S(2)}) copy-start(bf16[1,8,3584]{2,1,0:T(8,128)(2,1)} %param.6) | copy-start | bytes 172036
  0.6 35.2 %copy-start.1 = (f32[28,4,128]{2,1,0:T(4,128)S(1)}, f32[28,4,128]{2,1,0:T(4,128)}, u32[]{:S(2)}) copy-start(f32[28,4,128]{2,1,0:T(4,128)} %param.9) | copy-start | bytes 172036
  1.5 34.1 %collective-permute-start = (bf16[1,8,1]{2,1,0:T(8,128)(2,1)S(1)}, bf16[1,8,1]{2,1,0:T(8,128)(2,1)S(1)}, u32[]{:S(2)}, u32[]{:S(2)}) collective-permute-start(bf16[1,8,1]{2,1,0:T(8,128)(2,1)S(1)} %get-tuple-element.12), channel_id=1, source_target_pairs={{0,16},{16,32},{32,48},{48,64},{64,80},{80,96},{96,112},{112,128},... | collective-permute-start | bytes 56 | tf_op jit(solution)/shard_map/ppermute | solution.py:15
  6.6 28.9 %collective-permute-start.1 = (bf16[1,8,1]{2,1,0:T(8,128)(2,1)S(1)}, bf16[1,8,1]{2,1,0:T(8,128)(2,1)S(1)}, u32[]{:S(2)}, u32[]{:S(2)}) collective-permute-start(bf16[1,8,1]{2,1,0:T(8,128)(2,1)S(1)} %get-tuple-element.11), channel_id=1, source_target_pairs={{16,0},{32,16},{48,32},{64,48},{80,64},{96,80},{112,96},{128,112},... | collective-permute-start | bytes 56 | tf_op jit(solution)/shard_map/ppermute | solution.py:18
  26.3 22.7 %all-to-all-start.1 = ((f32[64,7,128]{2,1,0:T(8,128)}), f32[64,7,128]{2,1,0:T(8,128)S(1)}, u32[]{:S(2)}, u32[]{:S(2)}) async-start(f32[64,7,128]{2,1,0:T(8,128)} %copy.19), calls=%async_computation.1 | async-start | bytes 524288 | tf_op jit(solution)/shard_map/all_to_all | solution.py:81
  43.2 58.5 %copy-start.3 = (f32[4,896]{1,0:T(4,128)S(1)}, f32[4,896]{1,0:T(4,128)}, u32[]{:S(2)}) copy-start(f32[4,896]{1,0:T(4,128)} %param.11) | copy-start | bytes 43012
  48.9 52.6 %all-to-all-start = ((f32[64,7,8,128]{3,2,1,0:T(8,128)}), f32[64,7,8,128]{3,2,1,0:T(8,128)S(1)}, u32[]{:S(2)}, u32[]{:S(2)}) async-start(f32[64,7,8,128]{3,2,1,0:T(8,128)} %copy.18), calls=%async_computation | async-start | bytes 3670016 | tf_op jit(solution)/shard_map/all_to_all | solution.py:74
  149.5 54.4 %copy-start.2 = (f32[4,896]{1,0:T(4,128)}, f32[4,896]{1,0:T(4,128)S(1)}, u32[]{:S(2)}) copy-start(f32[4,896]{1,0:T(4,128)S(1)} %fusion.18) | copy-start | bytes 43012
where the time goes:
time: 204 us
  blocking collectives  96.2 us (47%)
  waiting for transfers between devices  51 us (25%)
  starting transfers between devices  35.6 us (17%)
  matrix products  9.53 us (5%)
  other arithmetic  5.56 us (3%)
  local copies, waits for them, and re-layouts  5.12 us (3%)
    all_gather x1, blocking collectives, shards(): all_states = lax.all_gather(ocean_next, 'cols', axis=1, tiled=True)  49.2 us
    psum x1, blocking collectives, shards(): flux_total = lax.psum(jnp.sum(sample_fluxes, axis=0), 'fld')  47 us
    all_to_all x1, waiting for transfers between devices, shards(): lax.all_to_all(outgoing.reshape(col_count, otiles, row_count, tile_len),...  45.3 us
    ppermute x1, starting transfers between devices, padded_2(): lax.ppermute(lax.slice_in_dim(block, 0, width, axis=dim), axis, backward)  14 us
    all_to_all x1, starting transfers between devices, shards(): lax.all_to_all(outgoing_area.reshape(col_count, otiles, tile_len), 'cols'...  9.31 us
    all_to_all x1, starting transfers between devices, shards(): lax.all_to_all(outgoing.reshape(col_count, otiles, row_count, tile_len),...  7.09 us
    all_to_all x1, waiting for transfers between devices, shards(): lax.all_to_all(outgoing_area.reshape(col_count, otiles, tile_len), 'cols'...  5.75 us
    ppermute x1, starting transfers between devices, padded_2(): lax.ppermute(lax.slice_in_dim(block, block.shape[dim] - width, None, axis...  5.18 us
  transfers between devices with their start and end apart: 4, of which 2 were waited for; matrix products, arithmetic and copies ran while one was open for 7% of the time, Pallas kernels for 0%

commit v1 on v0

v1 whole, which is shorter than its diff:
```python
import functools
import math

import jax
import jax.numpy as jnp
from jax import lax
from jax.experimental import pallas as pl
from jax.experimental.pallas import tpu as pltpu
from jax.sharding import PartitionSpec as P

TILE = 128
FIELDS = 8
MOST = 3
PAD = 32
MESH = pl.DeviceIdType.MESH
F32 = jnp.float32
BF16 = jnp.bfloat16


def split(x):
    high = x.astype(BF16)
    return high, (x - high.astype(F32)).astype(BF16)


def mixed(matrix, x):
    high, low = split(x)
    return jnp.dot(matrix, jnp.concatenate([high, low], axis=0), preferred_element_type=F32)


def kernel(
    ring, samples, tiles, reach, otiles, quarter,
    atm, owners, otile, cent, w_hbm, ocean,
    flux_out, ocean_out, atm_out,
    w, val, part, pick, pick_t, spread, oc, back,
    send1, recv1, send2, recv2, send3, recv3, send4, recv4, send5, recv5, send6, recv6,
    w_sem, halo_send, halo_recv, local_sem, ssem, rsem, osend, orecv,
):
    cols = ring * ring
    slots = MOST * ring
    rows = ring * slots
    entries = reach * PAD
    col = lax.axis_index("cols")
    fld = lax.axis_index("fld")
    x, z = col // ring, col % ring
    core = fld % 2
    first = (1 - core) * x + core * z
    second = (1 - core) * z + core * x

    def on_first(p):
        return ((1 - core) * (p * ring + second) + core * (second * ring + p), fld)

    def on_second(p):
        return ((1 - core) * (first * ring + p) + core * (p * ring + first), fld)

    def on_fld(p):
        return (col, p)

    left, right = (col + cols - 1) % cols, (col + 1) % cols

    chunk = 4 if tiles % 4 == 0 else 1
    chunks = tiles // chunk

    def weights(c):
        at = pl.ds(c * chunk, chunk)
        return pltpu.make_async_copy(w_hbm.at[at], w.at[at], w_sem.at[c])

    def start_weights(c, carry):
        weights(c).start()
        return carry

    lax.fori_loop(0, chunks, start_weights, 0)

    barrier = pltpu.get_barrier_semaphore()

    def greet(device):
        pl.semaphore_signal(barrier, inc=1, device_id=device, device_id_type=MESH)

    def greet_ring(d, carry):
        greet(on_first((first + d) % ring))
        greet(on_second((second + d) % ring))
        return carry

    def greet_fld(d, carry):
        greet(on_fld((fld + d) % samples))
        return carry

    greet((left, fld))
    greet((right, fld))
    lax.fori_loop(1, ring, greet_ring, 0)
    lax.fori_loop(1, samples, greet_fld, 0)

    def exchange(stage, count, me, device, source, target):
        def copy(d, to):
            return pltpu.make_async_remote_copy(
                src_ref=source((me + d) % count),
                dst_ref=target.at[to],
                send_sem=ssem.at[stage, d],
                recv_sem=rsem.at[stage, d],
                device_id=device((me + d) % count),
                device_id_type=MESH,
            )

        def send():
            def one(d, carry):
                copy(d, me).start()
                return carry

            lax.fori_loop(1, count, one, 0)

        def arrive():
            def one(d, carry):
                copy(d, (me + count - d) % count).wait_recv()
                return carry

            lax.fori_loop(1, count, one, 0)

        def leave():
            def one(d, carry):
                copy(d, me).wait_send()
                return carry

            lax.fori_loop(1, count, one, 0)

        return send, arrive, leave

    for t in range(tiles):
        val[t + 1] = atm[0, :, t * TILE : (t + 1) * TILE].astype(F32)
    for r in range(4):
        oc[r] = jnp.zeros((8, TILE), F32)
        for t in range(otiles):
            oc[r, t : t + 1, :] = ocean[r : r + 1, t * TILE : (t + 1) * TILE]
    part[...] = jnp.zeros_like(part)

    pl.semaphore_wait(barrier, 2 + 2 * (ring - 1) + samples - 1)
    to_right = pltpu.make_async_remote_copy(
        src_ref=val.at[tiles], dst_ref=val.at[0], send_sem=halo_send.at[0], recv_sem=halo_recv.at[0],
        device_id=(right, fld), device_id_type=MESH,
    )
    to_left = pltpu.make_async_remote_copy(
        src_ref=val.at[1], dst_ref=val.at[tiles + 1], send_sem=halo_send.at[1], recv_sem=halo_recv.at[1],
        device_id=(left, fld), device_id_type=MESH,
    )
    to_right.start()
    to_left.start()

    def down(ref, fill):
        table = jnp.concatenate([ref[...], jnp.full((PAD - tiles, reach), fill, jnp.int32)], axis=0)
        columns = [jnp.broadcast_to(table[:, k : k + 1], (PAD, entries)) for k in range(reach)]
        return jnp.concatenate(columns, axis=0).astype(F32)

    owner_down = down(owners, cols)
    owner_across = owner_down.T
    tile_across = down(otile, 0).T.astype(jnp.int32)
    at_row = lax.broadcasted_iota(jnp.int32, (entries, entries), 0)
    at_lane = lax.broadcasted_iota(jnp.int32, (entries, entries), 1)
    same = owner_down == owner_across
    rank_down = jnp.sum((same & (at_lane < at_row)).astype(F32), axis=1, keepdims=True).astype(jnp.int32)
    rank_across = jnp.sum((same & (at_row < at_lane)).astype(F32), axis=0, keepdims=True).astype(jnp.int32)

    def slot(owner, rank):
        owner = owner.astype(jnp.int32)
        high = owner // ring
        low = owner - high * ring
        group = (1 - core) * high + core * low
        place = (1 - core) * low + core * high
        return jnp.where(owner < cols, group * slots + rank * ring + place, -1)

    slot_across = slot(owner_across[:1], rank_across)
    slot_down = slot(owner_down[:, :1], rank_down)
    pick_f = (lax.broadcasted_iota(jnp.int32, (rows, entries), 0) == slot_across).astype(F32)
    pick[:, :entries] = pick_f.astype(BF16)
    pick[:, entries:] = pick_f.astype(BF16)
    pick_b = (lax.broadcasted_iota(jnp.int32, (entries, rows), 1) == slot_down).astype(F32).astype(BF16)
    pick_t[...] = pick_b
    named = jnp.sum(pick_f * (tile_across[:1] + 1).astype(F32), axis=1, keepdims=True)
    named = jnp.broadcast_to(named - 1.0, (rows, TILE))
    for g in range(ring):
        send1[g, (FIELDS + 1) * slots :] = named[g * slots : (g + 1) * slots]

    lane = lax.broadcasted_iota(jnp.int32, (FIELDS, TILE), 1)
    ones = jnp.ones((FIELDS, TILE), F32)

    def tile_sums(t):
        before, here, after = val[t], val[t + 1], val[t + 2]
        low = jnp.where(lane == 0, pltpu.roll(before, 1, 1), pltpu.roll(here, 1, 1))
        high = jnp.where(lane == TILE - 1, pltpu.roll(after, TILE - 1, 1), pltpu.roll(here, TILE - 1, 1))
        slope = 0.5 * (high - low)
        for k in range(reach):
            rebuilt = here + cent[t, k : k + 1, :] * slope
            operand = jnp.concatenate([rebuilt, ones], axis=0).astype(BF16)
            sums = lax.dot_general(
                operand, w[t, k], (((1,), (1,)), ((), ())), preferred_element_type=F32
            )
            part[pl.ds(k * PAD + t, FIELDS, stride=entries), :] = sums[:FIELDS]
            part[pl.ds(FIELDS * entries + k * PAD + t, 1), :] = sums[FIELDS : FIELDS + 1]

    def chunk_sums(c):
        weights(c).wait()
        for q in range(chunk):
            tile_sums(c * chunk + q)

    def inner(c, carry):
        chunk_sums(c)
        return carry

    lax.fori_loop(1, chunks - 1, inner, 0)
    to_right.wait_recv()
    to_left.wait_recv()

    def outer(c, carry):
        chunk_sums(c * (chunks - 1))
        return carry

    lax.fori_loop(0, 2, outer, 0)

    send, arrive, leave1 = exchange(0, ring, first, on_first, lambda p: send1.at[p], recv1)
    for f in range(FIELDS + 1):
        slotted = mixed(pick[...], part[f * entries : (f + 1) * entries])
        for g in range(ring):
            send1[g, f * slots : (f + 1) * slots] = slotted[g * slots : (g + 1) * slots]
    send()
    own = pltpu.make_async_copy(send1.at[first], recv1.at[first], local_sem.at[0])
    own.start()
    arrive()
    own.wait()

    row = lax.broadcasted_iota(jnp.int32, (rows, TILE), 0)
    target = recv1[:, (FIELDS + 1) * slots :].reshape(rows, TILE).astype(jnp.int32)
    member = (target >= 0) & (target + 8 * (row % ring) == lax.broadcasted_iota(jnp.int32, (rows, TILE), 1))
    member = member.astype(F32)
    gather = member.T[: 8 * ring].astype(BF16)
    spread[...] = member.astype(BF16)
    gather = jnp.concatenate([gather, gather], axis=1)
    send, arrive, leave2 = exchange(1, ring, second, on_second, lambda p: send2.at[p], recv2)
    for f in range(FIELDS + 1):
        dense = mixed(gather, recv1[:, f * slots : (f + 1) * slots].reshape(rows, TILE))
        send2[:, f] = dense.reshape(ring, 8, TILE)
    send()
    own = pltpu.make_async_copy(send2.at[second], recv2.at[second], local_sem.at[1])
    own.start()
    arrive()
    own.wait()

    total = recv2[0]
    for p in range(1, ring):
        total = total + recv2[p]
    forcing = total[:FIELDS] / jnp.maximum(total[FIELDS], 1.0)[None]

    sst, uo, vo = oc[0], oc[1], oc[2]
    slip_u = forcing[0] - uo
    slip_v = forcing[1] - vo
    wind_speed = jnp.sqrt(slip_u * slip_u + slip_v * slip_v + 0.25)
    saturation = 0.9 * jnp.exp(0.07 * sst - 0.1 * forcing[4])
    sensible = 0.4 * wind_speed * (sst - forcing[2])
    latent = 0.4 * wind_speed * (saturation - forcing[3])

    def softplus(v):
        return jnp.maximum(v, 0.0) + jnp.log1p(jnp.exp(-jnp.abs(v)))

    insolation = 0.5 + 1.5 * fld.astype(F32) / (samples - 1)
    net_heat = insolation * softplus(forcing[5]) + 0.3 * forcing[6] - 0.1 * sst - sensible - latent
    freshwater = softplus(forcing[7]) - latent
    stress_u = 0.5 * wind_speed * slip_u
    stress_v = 0.5 * wind_speed * slip_v
    send3[0] = net_heat
    send3[1] = stress_u
    send3[2] = stress_v
    send3[3] = -freshwater

    my_row = fld % 4
    send, arrive, leave3 = exchange(2, samples, fld, on_fld, lambda p: send3.at[p % 4], recv3)
    send()
    own = pltpu.make_async_copy(send3.at[my_row], recv3.at[fld], local_sem.at[2])
    own.start()
    for i, flux in enumerate((stress_u, stress_v, net_heat, freshwater)):
        flux_out[i] = flux
    arrive()
    own.wait()
    flux_sum = recv3[0]
    for p in range(1, samples):
        flux_sum = flux_sum + recv3[p]
    send4[...] = oc[my_row] + (0.5 / samples) * flux_sum

    send, arrive, leave4 = exchange(3, ring, second, on_second, lambda p: send4, recv4)
    send()
    mates = []
    for d in range(1, 4):
        mates.append(
            [
                pltpu.make_async_remote_copy(
                    src_ref=send4, dst_ref=ocean_row, send_sem=osend.at[d], recv_sem=orecv.at[d],
                    device_id=(col, (fld // 4) * 4 + (my_row + d) % 4), device_id_type=MESH,
                )
                for ocean_row in (back.at[my_row], back.at[(my_row + 4 - d) % 4])
            ]
        )
        mates[-1][0].start()
    recv4[second] = send4[...]
    back[my_row] = send4[...]
    arrive()

    states = recv4[...].reshape(ring * 8, TILE)
    scatter = spread[:, : ring * 8]
    slotted = mixed(jnp.concatenate([scatter, scatter], axis=1), states)
    for p in range(ring):
        send5[p] = slotted[p * slots : (p + 1) * slots]
    send, arrive, leave5 = exchange(4, ring, first, on_first, lambda p: send5.at[p], recv5)
    send()
    own = pltpu.make_async_copy(send5.at[first], recv5.at[first], local_sem.at[3])
    own.start()
    arrive()
    own.wait()
    pick_b = pick_t[...]
    part[:entries] = mixed(jnp.concatenate([pick_b, pick_b], axis=1), recv5[...].reshape(rows, TILE))

    begin = (fld // 4) * quarter
    row16 = lax.broadcasted_iota(jnp.int32, (16, TILE), 0)

    def remap(q, carry):
        t = begin + q
        state = part[pl.ds(t, reach, stride=PAD), :]
        high, low = split(state)
        high, low = high.astype(F32), low.astype(F32)
        sums = jnp.zeros((16, TILE), F32)
        for k in range(reach):
            operand = jnp.where(row16 == 0, high[k : k + 1], jnp.where(row16 == 1, low[k : k + 1], 1.0))
            sums = sums + jnp.dot(operand.astype(BF16), w[t, k], preferred_element_type=F32)
        send6[pl.ds(q, 1), :] = (sums[0:1] + sums[1:2]) / sums[2:3]
        return carry

    send6[...] = jnp.zeros_like(send6)
    lax.fori_loop(0, quarter, remap, 0)
    send, arrive, leave6 = exchange(5, samples, fld, on_fld, lambda p: send6, recv6)
    send()
    recv6[fld] = send6[...]
    for d in range(1, 4):
        mates[d - 1][1].wait_recv()
    ocean_out[...] = back[...]
    arrive()
    atm_out[...] = recv6[...]

    to_right.wait_send()
    to_left.wait_send()
    leave1()
    leave2()
    leave3()
    leave4()
    leave5()
    leave6()
    for d in range(1, 4):
        mates[d - 1][0].wait_send()


def shards(atm_state, owners, ocean_tile, centroid_offset, remap_weight, ocean_state):
    ring = math.isqrt(lax.axis_size("cols"))
    samples = lax.axis_size("fld")
    cells = atm_state.shape[2]
    tiles = cells // TILE
    reach = owners.shape[1]
    ocells = ocean_state.shape[1]
    otiles = ocells // TILE
    slots = MOST * ring
    rows = ring * slots
    entries = reach * PAD
    groups = samples // 4
    quarter = -(-tiles // groups)
    sent = (FIELDS + 2) * slots
    most = max(ring, samples)
    vmem = pl.BlockSpec(memory_space=pltpu.VMEM)
    fluxes, ocean, back = pl.pallas_call(
        functools.partial(kernel, ring, samples, tiles, reach, otiles, quarter),
        out_shape=(
            jax.ShapeDtypeStruct((4, 8, TILE), F32),
            jax.ShapeDtypeStruct((4, 8, TILE), F32),
            jax.ShapeDtypeStruct((samples, 8, TILE), F32),
        ),
        in_specs=[vmem, vmem, vmem, vmem, pl.BlockSpec(memory_space=pl.ANY), vmem],
        out_specs=(vmem, vmem, vmem),
        scratch_shapes=[
            pltpu.VMEM((tiles, reach, TILE, TILE), BF16),
            pltpu.VMEM((tiles + 2, FIELDS, TILE), F32),
            pltpu.VMEM(((FIELDS + 1) * entries, TILE), F32),
            pltpu.VMEM((rows, 2 * entries), BF16),
            pltpu.VMEM((entries, rows), BF16),
            pltpu.VMEM((rows, TILE), BF16),
            pltpu.VMEM((4, 8, TILE), F32),
            pltpu.VMEM((4, 8, TILE), F32),
            pltpu.VMEM((ring, sent, TILE), F32),
            pltpu.VMEM((ring, sent, TILE), F32),
            pltpu.VMEM((ring, FIELDS + 1, 8, TILE), F32),
            pltpu.VMEM((ring, FIELDS + 1, 8, TILE), F32),
            pltpu.VMEM((4, 8, TILE), F32),
            pltpu.VMEM((samples, 8, TILE), F32),
            pltpu.VMEM((8, TILE), F32),
            pltpu.VMEM((ring, 8, TILE), F32),
            pltpu.VMEM((ring, slots, TILE), F32),
            pltpu.VMEM((ring, slots, TILE), F32),
            pltpu.VMEM((8, TILE), F32),
            pltpu.VMEM((samples, 8, TILE), F32),
            pltpu.SemaphoreType.DMA((tiles,)),
            pltpu.SemaphoreType.DMA((2,)),
            pltpu.SemaphoreType.DMA((2,)),
            pltpu.SemaphoreType.DMA((4,)),
            pltpu.SemaphoreType.DMA((6, most)),
            pltpu.SemaphoreType.DMA((6, most)),
            pltpu.SemaphoreType.DMA((4,)),
            pltpu.SemaphoreType.DMA((4,)),
        ],
        compiler_params=pltpu.CompilerParams(
            collective_id=0, has_side_effects=True, vmem_limit_bytes=32 * 1024 * 1024
        ),
        name="coupling",
    )(atm_state, owners, ocean_tile, centroid_offset, remap_weight, ocean_state)
    sample_fluxes = fluxes[:, :otiles].reshape(1, 4, ocells)
    ocean_next = ocean[:, :otiles].reshape(4, ocells)
    atm_surface = back.reshape(groups, 4, 8, TILE)[:, :, :quarter].transpose(1, 0, 2, 3)
    return sample_fluxes, ocean_next, atm_surface.reshape(4, groups * quarter * TILE)[:, :cells]


def solution(mesh):
    return jax.shard_map(
        shards,
        mesh=mesh,
        in_specs=(
            P("fld", None, "cols"),
            P("cols", None),
            P("cols", None),
            P("cols", None, None),
            P("cols", None, None, None),
            P(None, "cols"),
        ),
        out_specs=(P("fld", None, "cols"), P(None, "cols"), P(None, "cols")),
        check_vma=False,
    )
```

time: 204 us -> 83.7 us (0.41)
  the two profiles are of different devices: /device:TPU:4 before, /device:TPU:1 now
where the time goes in v1:
time: 83.7 us; the launch traced here: 83.4 us
  Pallas kernels  74.9 us (89%)
  local copies, waits for them, and re-layouts  7.81 us (9%)
    pallas_call x1, Pallas kernels, shards(): pl.pallas_call(functools.partial(kernel, ring, samples, tiles, reach, oti...  74.9 us
    unnamed x12, local copies, waits for them, and re-layouts  6.54 us

profile of v1, /device:TPU:1, one launch (start us, length us, event | category | flops | bytes accessed | tf_op | source)
XLA Modules:
  0.0 83.4 jit_solution(7521226397611476856)
XLA Ops:
  0.6 0.8 copy.12.owners
  1.4 0.8 copy.13.otile
  2.2 0.0 copy-start
  2.2 2.0 %copy-done = bf16[28,4,128,128]{3,2,1,0:T(8,128)(2,1)S(1)} copy-done((bf16[28,4,128,128]{3,2,1,0:T(8,128)(2,1)S(1)}, bf16[28,4,128,128]{3,2,1,0:T(8,128)(2,1)}, u32[]{:S(2)}) %copy-start) | copy-done | bytes 3670040
  4.2 0.0 copy-start.1
  4.2 0.8 copy-done.1
  5.0 0.0 copy-start.2
  5.0 0.8 copy-done.2
  5.9 0.0 copy-start.3
  5.9 0.7 copy-done.3
  6.6 74.9 %coupling.1 = (f32[4,8,128]{2,1,0:T(8,128)S(1)}, f32[4,8,128]{2,1,0:T(8,128)S(1)}, f32[16,8,128]{2,1,0:T(8,128)S(1)}) custom-call(bf16[1,8,3584]{2,1,0:T(8,128)(2,1)S(1)} %copy-done.1, s32[28,4]{1,0:T(8,128)S(1)} %copy.12.owners, s32[28,4]{1,0:T(8,128)S(1)} %copy.13.otile, f32[28,4,128]{2,1,0:T(4,128)S(1)} %copy-done.2, ...), custom_call_target="tpu_custom_call" | custom-call | tf_op jit(solution)/shard_map/coupling/pallas_call | solution.py:370
  81.5 0.6 reshape.18
  82.1 0.6 copy.19
  82.7 0.6 reshape.21
  (2 shorter events, 0.0 us)
Async XLA Ops:
  2.2 2.0 %copy-start = (bf16[28,4,128,128]{3,2,1,0:T(8,128)(2,1)S(1)}, bf16[28,4,128,128]{3,2,1,0:T(8,128)(2,1)}, u32[]{:S(2)}) copy-start(bf16[28,4,128,128]{3,2,1,0:T(8,128)(2,1)} %w_hbm.1) | copy-start | bytes 11010052
  4.2 0.8 copy-start.1
  5.0 0.8 copy-start.2
  5.9 0.7 copy-start.3

commit v2 on v1

v2 whole, which is shorter than its diff:
```python
import functools
import math

import jax
import jax.numpy as jnp
from jax import lax
from jax.experimental import pallas as pl
from jax.experimental.pallas import tpu as pltpu
from jax.sharding import PartitionSpec as P

TILE = 128
FIELDS = 8
MOST = 3
PAD = 32
LEVELS = 5400.0
LEAST = 1e-30
MESH = pl.DeviceIdType.MESH
F32 = jnp.float32
BF16 = jnp.bfloat16
I32 = jnp.int32
I16 = jnp.int16


def split(x):
    high = x.astype(BF16)
    return high, (x - high.astype(F32)).astype(BF16)


def mixed(matrix, x):
    high, low = split(x)
    return jnp.dot(matrix, jnp.concatenate([high, low], axis=0), preferred_element_type=F32)


def twice(matrix):
    return jnp.concatenate([matrix, matrix], axis=1)


def kernel(
    ring, samples, tiles, reach, otiles,
    atm_hbm, owners_hbm, otile_hbm, cent_hbm, w_hbm, ocean_hbm,
    flux_out, ocean_out, atm_out,
    atm, owners, otile, cent, w, ocean,
    val, part, pick, pick_t, spread, oc, table, col_inverse, lhs,
    send0, recv0, send1a, recv1a, send1, recv1, send2a, recv2a, send2, recv2,
    send3, recv3, send3y, recv3y, send4, recv4, send5, recv5,
    in_sem, w_sem, halo_send, halo_recv, ssem, rsem, psend, precv,
):
    cols = ring * ring
    chips = samples // 2
    slots = MOST * ring
    rows = ring * slots
    entries = reach * PAD
    col = lax.axis_index("cols")
    fld = lax.axis_index("fld")
    x, z = col // ring, col % ring
    chip, core = fld // 2, fld % 2
    first = (1 - core) * x + core * z
    second = (1 - core) * z + core * x

    def on_first(p):
        return ((1 - core) * (p * ring + second) + core * (second * ring + p), fld)

    def on_second(p):
        return ((1 - core) * (first * ring + p) + core * (p * ring + first), fld)

    def on_chip(p):
        return (col, p * 2 + core)

    sibling = (col, chip * 2 + 1 - core)
    left, right = (col + cols - 1) % cols, (col + 1) % cols

    barrier = pltpu.get_barrier_semaphore()

    def greet(device):
        pl.semaphore_signal(barrier, inc=1, device_id=device, device_id_type=MESH)

    def greet_ring(d, carry):
        greet(on_first((first + d) % ring))
        greet(on_second((second + d) % ring))
        return carry

    def greet_chip(d, carry):
        greet(on_chip((chip + d) % chips))
        return carry

    greet((left, fld))
    greet((right, fld))
    greet(sibling)
    lax.fori_loop(1, ring, greet_ring, 0)
    lax.fori_loop(1, chips, greet_chip, 0)

    small = [
        pltpu.make_async_copy(source, target, in_sem.at[i])
        for i, (source, target) in enumerate(
            ((atm_hbm, atm), (owners_hbm, owners), (otile_hbm, otile), (cent_hbm, cent), (ocean_hbm, ocean))
        )
    ]
    for copy in small:
        copy.start()
    chunk = 4 if tiles % 4 == 0 else 1
    chunks = tiles // chunk

    def weights(c):
        at = pl.ds(c * chunk, chunk)
        return pltpu.make_async_copy(w_hbm.at[at], w.at[at], w_sem.at[c])

    def start_weights(c, carry):
        weights(c).start()
        return carry

    lax.fori_loop(0, chunks, start_weights, 0)

    def exchange(stage, count, me, device, source, target):
        def copy(d, to):
            return pltpu.make_async_remote_copy(
                src_ref=source((me + d) % count),
                dst_ref=target.at[to],
                send_sem=ssem.at[stage, d],
                recv_sem=rsem.at[stage, d],
                device_id=device((me + d) % count),
                device_id_type=MESH,
            )

        def send():
            for d in sorted(range(1, count), key=lambda d: -min(d, count - d)):
                copy(d, me).start()

        def arrive():
            def one(d, carry):
                copy(d, (me + count - d) % count).wait_recv()
                return carry

            lax.fori_loop(1, count, one, 0)

        def leave():
            def one(d, carry):
                copy(d, me).wait_send()
                return carry

            lax.fori_loop(1, count, one, 0)

        return send, arrive, leave

    def to_sibling(i, source, target):
        return pltpu.make_async_remote_copy(
            src_ref=source, dst_ref=target, send_sem=psend.at[i], recv_sem=precv.at[i],
            device_id=sibling, device_id_type=MESH,
        )

    part[...] = jnp.zeros_like(part)
    col_inverse[...] = jnp.ones_like(col_inverse)
    small[0].wait()
    for t in range(tiles):
        val[t + 1] = atm[0, :, t * TILE : (t + 1) * TILE].astype(F32)
    to_right = pltpu.make_async_remote_copy(
        src_ref=val.at[tiles], dst_ref=val.at[0], send_sem=halo_send.at[0], recv_sem=halo_recv.at[0],
        device_id=(right, fld), device_id_type=MESH,
    )
    to_left = pltpu.make_async_remote_copy(
        src_ref=val.at[1], dst_ref=val.at[tiles + 1], send_sem=halo_send.at[1], recv_sem=halo_recv.at[1],
        device_id=(left, fld), device_id_type=MESH,
    )
    pl.semaphore_wait(barrier, 3 + 2 * (ring - 1) + chips - 1)
    to_right.start()
    to_left.start()

    small[1].wait()
    small[2].wait()
    lane = lax.broadcasted_iota(I32, (FIELDS, TILE), 1)

    def across(ref, fill):
        table[...] = jnp.full((8, TILE), fill, F32)
        table[:reach, :tiles] = ref[...].astype(F32)
        line = jnp.broadcast_to(table[0:1], (8, TILE))
        for k in range(1, reach):
            shifted = pltpu.roll(jnp.broadcast_to(table[k : k + 1], (8, TILE)), k * PAD, 1)
            line = jnp.where(lane >= k * PAD, shifted, line)
        return line[:1]

    owner_across = across(owners, float(cols))
    tile_across = across(otile, 0.0)
    owner_down = jnp.broadcast_to(owner_across, (entries, entries)).T
    at_row = lax.broadcasted_iota(I32, (entries, entries), 0)
    at_lane = lax.broadcasted_iota(I32, (entries, entries), 1)
    same = owner_down == owner_across
    rank_down = jnp.sum((same & (at_lane < at_row)).astype(F32), axis=1, keepdims=True).astype(I32)
    rank_across = jnp.sum((same & (at_row < at_lane)).astype(F32), axis=0, keepdims=True).astype(I32)

    def slot(owner, rank):
        owner = owner.astype(I32)
        high = owner // ring
        low = owner - high * ring
        group = (1 - core) * high + core * low
        place = (1 - core) * low + core * high
        return jnp.where(owner < cols, group * slots + rank * ring + place, -1)

    slot_across = slot(owner_across, rank_across)
    slot_down = slot(owner_down[:, :1], rank_down)
    pick_f = (lax.broadcasted_iota(I32, (rows, entries), 0) == slot_across).astype(F32)
    pick[...] = twice(pick_f.astype(BF16))
    pick_b = (lax.broadcasted_iota(I32, (entries, rows), 1) == slot_down).astype(F32).astype(BF16)
    pick_t[...] = twice(pick_b)
    named = jnp.sum(pick_f * (tile_across + 1.0), axis=1, keepdims=True)
    named = jnp.broadcast_to(named - 1.0, (rows, TILE))
    for g in range(ring):
        send0[g] = named[g * slots : (g + 1) * slots]
    send, arrive0, leave0 = exchange(0, ring, first, on_first, lambda p: send0.at[p], recv0)
    send()
    recv0[first] = send0[first]

    small[4].wait()
    for r in range(4):
        oc[r] = jnp.zeros((8, TILE), F32)
        for t in range(otiles):
            oc[r, t : t + 1, :] = ocean[r : r + 1, t * TILE : (t + 1) * TILE]

    ones = jnp.ones((FIELDS, TILE), F32)
    small[3].wait()

    def tile_sums(t):
        before, here, after = val[t], val[t + 1], val[t + 2]
        low = jnp.where(lane == 0, pltpu.roll(before, 1, 1), pltpu.roll(here, 1, 1))
        high = jnp.where(lane == TILE - 1, pltpu.roll(after, TILE - 1, 1), pltpu.roll(here, TILE - 1, 1))
        slope = 0.5 * (high - low)
        for k in range(reach):
            rebuilt = here + cent[t, k : k + 1, :] * slope
            operand = jnp.concatenate([rebuilt, ones], axis=0).astype(BF16)
            sums = lax.dot_general(
                operand, w[t, k], (((1,), (1,)), ((), ())), preferred_element_type=F32
            )
            area = sums[FIELDS : FIELDS + 1]
            code = jnp.round(sums[:FIELDS] * (LEVELS / jnp.maximum(area, LEAST)))
            part[pl.ds(k * PAD + t, FIELDS, stride=entries), :] = code
            part[pl.ds(FIELDS * entries + k * PAD + t, 1), :] = area

    def chunk_sums(c):
        weights(c).wait()
        for q in range(chunk):
            tile_sums(c * chunk + q)

    def inner(c, carry):
        chunk_sums(c)
        return carry

    lax.fori_loop(1, chunks - 1, inner, 0)
    to_right.wait_recv()
    to_left.wait_recv()

    def outer(c, carry):
        chunk_sums(c * (chunks - 1))
        return carry

    lax.fori_loop(0, 2, outer, 0)

    send, arrive1a, leave1a = exchange(1, ring, first, on_first, lambda p: send1a.at[p], recv1a)
    slotted = mixed(pick[...], part[FIELDS * entries :])
    for g in range(ring):
        send1a[g] = slotted[g * slots : (g + 1) * slots]
    send()
    send, arrive1, leave1 = exchange(2, ring, first, on_first, lambda p: send1.at[p], recv1)
    for f in range(0, FIELDS, 2):
        one = mixed(pick[...], part[f * entries : (f + 1) * entries])
        two = mixed(pick[...], part[(f + 1) * entries : (f + 2) * entries])
        for g in range(ring):
            at = slice(g * slots, (g + 1) * slots)
            pair = jnp.concatenate([one[at], two[at]], axis=0)
            send1[g, f * slots : (f + 2) * slots] = pair.astype(I32).astype(I16)
    send()
    recv1a[first] = send1a[first]
    recv1[first] = send1[first]

    arrive0()
    row = lax.broadcasted_iota(I32, (rows, TILE), 0)
    target = recv0[...].reshape(rows, TILE).astype(I32)
    member = (target >= 0) & (target + 8 * (row % ring) == lax.broadcasted_iota(I32, (rows, TILE), 1))
    member = member.astype(F32)
    gather = twice(member.T[: 8 * ring].astype(BF16))
    spread[...] = twice(member[:, : 8 * ring].astype(BF16))
    all_ones = jnp.ones((16, reach * TILE), BF16)

    def column_area(c, carry):
        for q in range(chunk):
            t = c * chunk + q
            area = jnp.dot(all_ones, w[t].reshape(reach * TILE, TILE), preferred_element_type=F32)
            col_inverse[pl.ds(t, 1), :] = 1.0 / area[:1]
        return carry

    lax.fori_loop(0, chunks, column_area, 0)

    send, arrive2a, leave2a = exchange(3, ring, second, on_second, lambda p: send2a.at[p], recv2a)
    arrive1a()
    areas = recv1a[...].reshape(rows, TILE)
    dense_area = mixed(gather, areas)
    send2a[...] = dense_area.reshape(ring, 8, TILE)
    send()
    per_area = 1.0 / jnp.maximum(dense_area, LEAST)
    send, arrive2, leave2 = exchange(4, ring, second, on_second, lambda p: send2.at[p], recv2)
    arrive1()
    for f in range(0, FIELDS, 2):
        pair = recv1[:, f * slots : (f + 2) * slots].astype(I32).astype(F32)
        one = mixed(gather, pair[:, :slots].reshape(rows, TILE) * areas) * per_area
        two = mixed(gather, pair[:, slots:].reshape(rows, TILE) * areas) * per_area
        both = jnp.concatenate([one.reshape(ring, 8, TILE), two.reshape(ring, 8, TILE)], axis=1)
        send2[:, f * 8 : (f + 2) * 8] = jnp.round(both).astype(I32).astype(I16)
    send()
    recv2a[second] = send2a[second]
    recv2[second] = send2[second]
    arrive2a()
    arrive2()

    coverage = jnp.zeros((8, TILE), F32)
    total = jnp.zeros((FIELDS, 8, TILE), F32)
    for p in range(ring):
        area = recv2a[p]
        coverage = coverage + area
        total = total + recv2[p].astype(I32).astype(F32).reshape(FIELDS, 8, TILE) * area[None]
    forcing = total * (1.0 / (LEVELS * jnp.maximum(coverage, 1.0)))[None]

    sst, uo, vo = oc[0], oc[1], oc[2]
    slip_u = forcing[0] - uo
    slip_v = forcing[1] - vo
    wind_speed = jnp.sqrt(slip_u * slip_u + slip_v * slip_v + 0.25)
    saturation = 0.9 * jnp.exp(0.07 * sst - 0.1 * forcing[4])
    sensible = 0.4 * wind_speed * (sst - forcing[2])
    latent = 0.4 * wind_speed * (saturation - forcing[3])

    def softplus(v):
        return jnp.maximum(v, 0.0) + jnp.log1p(jnp.exp(-jnp.abs(v)))

    insolation = 0.5 + 1.5 * fld.astype(F32) / (samples - 1)
    net_heat = insolation * softplus(forcing[5]) + 0.3 * forcing[6] - 0.1 * sst - sensible - latent
    freshwater = softplus(forcing[7]) - latent
    stress_u = 0.5 * wind_speed * slip_u
    stress_v = 0.5 * wind_speed * slip_v
    send3[0] = net_heat
    send3[1] = stress_u
    send3[2] = stress_v
    send3[3] = -freshwater

    mine, other = pl.ds(2 * core, 2), pl.ds(2 - 2 * core, 2)
    pair_copy = to_sibling(0, send3.at[other], recv3)
    pair_copy.start()
    for i, flux in enumerate((stress_u, stress_v, net_heat, freshwater)):
        flux_out[i] = flux
    pair_copy.wait_recv()
    send3y[...] = send3[mine] + recv3[...]
    send, arrive, leave3 = exchange(5, chips, chip, on_chip, lambda p: send3y, recv3y)
    send()
    recv3y[chip] = send3y[...]
    arrive()
    flux_sum = recv3y[0]
    for p in range(1, chips):
        flux_sum = flux_sum + recv3y[p]
    state = oc[mine] + (0.5 / samples) * flux_sum
    send4[...] = state

    send, arrive, leave4 = exchange(6, ring, second, on_second, lambda p: send4, recv4)
    send()
    recv4[second] = state
    ocean_out[mine] = state
    ocean_copy = to_sibling(1, ocean_out.at[mine], ocean_out.at[mine])
    ocean_copy.start()
    arrive()

    states = [recv4[:, r].reshape(ring * 8, TILE) for r in range(2)]
    slotted = mixed(spread[...], jnp.concatenate(states, axis=1))
    for p in range(ring):
        for r in range(2):
            send5[p, r] = slotted[p * slots : (p + 1) * slots, r * TILE : (r + 1) * TILE]
    send, arrive, leave5 = exchange(7, ring, first, on_first, lambda p: send5.at[p], recv5)
    send()
    recv5[first] = send5[first]
    arrive()

    states = [recv5[:, r].reshape(rows, TILE) for r in range(2)]
    entry = mixed(pick_t[...], jnp.concatenate(states, axis=1))
    high, low = split(entry)
    high, low = high.astype(F32), low.astype(F32)
    for k in range(reach):
        for j in range(PAD // 8):
            at = slice(k * PAD + j * 8, k * PAD + j * 8 + 8)
            block = [high[at, :TILE], low[at, :TILE], high[at, TILE:], low[at, TILE:]]
            lhs[j, :, k * TILE : (k + 1) * TILE] = jnp.concatenate(block, axis=0).astype(BF16)

    row8 = lax.broadcasted_iota(I32, (8, TILE), 0)

    def results(j):
        at = pl.ds(j * 8, 8)
        return to_sibling(2 + j, atm_out.at[mine, at], atm_out.at[mine, at])

    def remap(j, count):
        operand = lhs[j]
        one = two = jnp.zeros((8, TILE), F32)
        for q in range(count):
            sums = jnp.dot(operand, w[j * 8 + q].reshape(reach * TILE, TILE), preferred_element_type=F32)
            one = jnp.where(row8 == q, sums[0:8] + sums[8:16], one)
            two = jnp.where(row8 == q, sums[16:24] + sums[24:32], two)
        at = pl.ds(j * 8, 8)
        inverse = col_inverse[at]
        atm_out[2 * core, at] = one * inverse
        atm_out[2 * core + 1, at] = two * inverse
        results(j).start()

    def full_remap(j, carry):
        remap(j, 8)
        return carry

    whole, rest = tiles // 8, tiles % 8
    lax.fori_loop(0, whole, full_remap, 0)
    if rest:
        remap(whole, rest)
    blocks = whole + (rest > 0)

    def finish(j, carry):
        at = pl.ds(j * 8, 8)
        to_sibling(2 + j, atm_out.at[mine, at], atm_out.at[other, at]).wait_recv()
        results(j).wait_send()
        return carry

    lax.fori_loop(0, blocks, finish, 0)
    to_sibling(1, ocean_out.at[mine], ocean_out.at[other]).wait_recv()
    ocean_copy.wait_send()
    pair_copy.wait_send()
    to_right.wait_send()
    to_left.wait_send()
    for leave in (leave0, leave1a, leave1, leave2a, leave2, leave3, leave4, leave5):
        leave()


def shards(atm_state, owners, ocean_tile, centroid_offset, remap_weight, ocean_state):
    ring = math.isqrt(lax.axis_size("cols"))
    samples = lax.axis_size("fld")
    cells = atm_state.shape[2]
    tiles = cells // TILE
    reach = owners.shape[1]
    ocells = ocean_state.shape[1]
    otiles = ocells // TILE
    chips = samples // 2
    slots = MOST * ring
    rows = ring * slots
    entries = reach * PAD
    most = max(ring, chips)
    hbm = pl.BlockSpec(memory_space=pltpu.HBM)
    vmem = pl.BlockSpec(memory_space=pltpu.VMEM)
    fluxes, ocean, back = pl.pallas_call(
        functools.partial(kernel, ring, samples, tiles, reach, otiles),
        out_shape=(
            jax.ShapeDtypeStruct((4, 8, TILE), F32),
            jax.ShapeDtypeStruct((4, 8, TILE), F32),
            jax.ShapeDtypeStruct((4, PAD, TILE), F32),
        ),
        in_specs=[hbm] * 6,
        out_specs=(vmem, vmem, vmem),
        scratch_shapes=[
            pltpu.VMEM(atm_state.shape, BF16),
            pltpu.VMEM((reach, tiles), I32),
            pltpu.VMEM((reach, tiles), I32),
            pltpu.VMEM((tiles, reach, TILE), F32),
            pltpu.VMEM((tiles, reach, TILE, TILE), BF16),
            pltpu.VMEM((4, ocells), F32),
            pltpu.VMEM((tiles + 2, FIELDS, TILE), F32),
            pltpu.VMEM(((FIELDS + 1) * entries, TILE), F32),
            pltpu.VMEM((rows, 2 * entries), BF16),
            pltpu.VMEM((entries, 2 * rows), BF16),
            pltpu.VMEM((rows, 16 * ring), BF16),
            pltpu.VMEM((4, 8, TILE), F32),
            pltpu.VMEM((8, TILE), F32),
            pltpu.VMEM((PAD, TILE), F32),
            pltpu.VMEM((PAD // 8, 32, reach * TILE), BF16),
            pltpu.VMEM((ring, slots, TILE), F32),
            pltpu.VMEM((ring, slots, TILE), F32),
            pltpu.VMEM((ring, slots, TILE), F32),
            pltpu.VMEM((ring, slots, TILE), F32),
            pltpu.VMEM((ring, FIELDS * slots, TILE), I16),
            pltpu.VMEM((ring, FIELDS * slots, TILE), I16),
            pltpu.VMEM((ring, 8, TILE), F32),
            pltpu.VMEM((ring, 8, TILE), F32),
            pltpu.VMEM((ring, FIELDS * 8, TILE), I16),
            pltpu.VMEM((ring, FIELDS * 8, TILE), I16),
            pltpu.VMEM((4, 8, TILE), F32),
            pltpu.VMEM((2, 8, TILE), F32),
            pltpu.VMEM((2, 8, TILE), F32),
            pltpu.VMEM((chips, 2, 8, TILE), F32),
            pltpu.VMEM((2, 8, TILE), F32),
            pltpu.VMEM((ring, 2, 8, TILE), F32),
            pltpu.VMEM((ring, 2, slots, TILE), F32),
            pltpu.VMEM((ring, 2, slots, TILE), F32),
            pltpu.SemaphoreType.DMA((5,)),
            pltpu.SemaphoreType.DMA((tiles,)),
            pltpu.SemaphoreType.DMA((2,)),
            pltpu.SemaphoreType.DMA((2,)),
            pltpu.SemaphoreType.DMA((8, most)),
            pltpu.SemaphoreType.DMA((8, most)),
            pltpu.SemaphoreType.DMA((2 + PAD // 8,)),
            pltpu.SemaphoreType.DMA((2 + PAD // 8,)),
        ],
        compiler_params=pltpu.CompilerParams(
            collective_id=0, has_side_effects=True, vmem_limit_bytes=60 * 1024 * 1024
        ),
        name="coupling",
    )(atm_state, owners.T, ocean_tile.T, centroid_offset, remap_weight, ocean_state)
    sample_fluxes = fluxes[:, :otiles].reshape(1, 4, ocells)
    ocean_next = ocean[:, :otiles].reshape(4, ocells)
    return sample_fluxes, ocean_next, back[:, :tiles].reshape(4, cells)


def solution(mesh):
    return jax.shard_map(
        shards,
        mesh=mesh,
        in_specs=(
            P("fld", None, "cols"),
            P("cols", None),
            P("cols", None),
            P("cols", None, None),
            P("cols", None, None, None),
            P(None, "cols"),
        ),
        out_specs=(P("fld", None, "cols"), P(None, "cols"), P(None, "cols")),
        check_vma=False,
    )
```

time: 83.7 us -> 67.6 us (0.81)
  Pallas kernels: 74.9 us -> 62.4 us
  local copies, waits for them, and re-layouts: 7.81 us -> 4.16 us
    pallas_call x1, Pallas kernels: 74.9 us -> 62.4 us  [shards(): pl.pallas_call(functools.partial(kernel, ring, samples, tiles, reach, oti...]
    unnamed x12 -> x4, local copies, waits for them, and re-layouts: 6.54 us -> 2.83 us
where the time goes in v2:
time: 67.6 us; the launch traced here: 67.2 us
  Pallas kernels  62.4 us (92%)
  local copies, waits for them, and re-layouts  4.16 us (6%)
    pallas_call x1, Pallas kernels, shards(): pl.pallas_call(functools.partial(kernel, ring, samples, tiles, reach, oti...  62.4 us
    unnamed x4, local copies, waits for them, and re-layouts  2.83 us

profile of v2, /device:TPU:1, one launch (start us, length us, event | category | flops | bytes accessed | tf_op | source)
XLA Modules:
  0.0 67.2 jit_solution(5121136820751764469)
XLA Ops:
  0.6 62.4 %coupling.1 = (f32[4,8,128]{2,1,0:T(8,128)}, f32[4,8,128]{2,1,0:T(8,128)}, f32[4,32,128]{2,1,0:T(8,128)}) custom-call(bf16[1,8,3584]{2,1,0:T(8,128)(2,1)} %atm_hbm.1, s32[4,28]{1,0:T(4,128)} %bitcast.16, s32[4,28]{1,0:T(4,128)} %bitcast.17, f32[28,4,128]{2,1,0:T(4,128)} %cent_hbm.1, bf16[28,4,128,128]{3,2,1,0:T(8,128)(2,1)} %w_hbm.1, f32[4,896]{1,0:T(4,128)} %ocean_hbm.1), custom_call_target="tpu_custom_call" | custom-call | tf_op jit(solution)/shard_map/coupling/pallas_call | solution.py:445
  63.1 1.3 %reshape.15 = f32[1,4,896]{2,1,0:T(4,128)} reshape(f32[4,7,128]{2,1,0:T(8,128)} %bitcast.14) | data formatting | bytes 28672 | tf_op jit(solution)/shard_map/reshape | solution.py:502
  64.4 0.7 %slice_bitcast_fusion.1 = f32[1,4,7,128]{3,2,1,0:T(8,128)S(1)} fusion(f32[4,8,128]{2,1,0:T(8,128)} %get-tuple-element.7), kind=kLoop, calls=%fused_computation.2 | loop fusion | bytes 28672
  65.1 0.6 copy.14
  65.7 0.8 %slice_bitcast_fusion = f32[1,4,28,128]{3,2,1,0:T(8,128)S(1)} fusion(f32[4,32,128]{2,1,0:T(8,128)} %get-tuple-element.8), kind=kLoop, calls=%fused_computation | loop fusion | bytes 114688
  66.6 0.7 copy.13

commit v3 on v2

--- a/solution.py
+++ b/solution.py
@@ -38,12 +38,13 @@
 def kernel(
     ring, samples, tiles, reach, otiles,
     atm_hbm, owners_hbm, otile_hbm, cent_hbm, w_hbm, ocean_hbm,
+    flux_hbm, ocean_next_hbm, back_hbm,
     flux_out, ocean_out, atm_out,
-    atm, owners, otile, cent, w, ocean,
+    rows_next, rows_back, atm, owners, otile, cent, w, ocean,
     val, part, pick, pick_t, spread, oc, table, col_inverse, lhs,
     send0, recv0, send1a, recv1a, send1, recv1, send2a, recv2a, send2, recv2,
     send3, recv3, send3y, recv3y, send4, recv4, send5, recv5,
-    in_sem, w_sem, halo_send, halo_recv, ssem, rsem, psend, precv,
+    in_sem, out_sem, w_sem, halo_send, halo_recv, ssem, rsem, psend, precv,
 ):
     cols = ring * ring
     chips = samples // 2
@@ -74,20 +75,17 @@
     def greet(device):
         pl.semaphore_signal(barrier, inc=1, device_id=device, device_id_type=MESH)
 
-    def greet_ring(d, carry):
+    def far_first(count):
+        return sorted(range(1, count), key=lambda d: -min(d, count - d))
+
+    for d in far_first(ring):
         greet(on_first((first + d) % ring))
         greet(on_second((second + d) % ring))
-        return carry
-
-    def greet_chip(d, carry):
+    for d in far_first(chips):
         greet(on_chip((chip + d) % chips))
-        return carry
-
     greet((left, fld))
     greet((right, fld))
     greet(sibling)
-    lax.fori_loop(1, ring, greet_ring, 0)
-    lax.fori_loop(1, chips, greet_chip, 0)
 
     small = [
         pltpu.make_async_copy(source, target, in_sem.at[i])
@@ -97,49 +95,34 @@
     ]
     for copy in small:
         copy.start()
-    chunk = 4 if tiles % 4 == 0 else 1
-    chunks = tiles // chunk
+    groups, rest = (tiles - 2) // 4, (tiles - 2) % 4
+    spans = [(1 + 4 * c, 4) for c in range(groups)] + [(1 + 4 * groups, rest + 1), (0, 1)]
 
     def weights(c):
-        at = pl.ds(c * chunk, chunk)
+        at = pl.ds(*spans[c]) if isinstance(c, int) else pl.ds(1 + 4 * c, 4)
         return pltpu.make_async_copy(w_hbm.at[at], w.at[at], w_sem.at[c])
 
-    def start_weights(c, carry):
+    for c in range(groups + 2):
         weights(c).start()
-        return carry
-
-    lax.fori_loop(0, chunks, start_weights, 0)
 
     def exchange(stage, count, me, device, source, target):
-        def copy(d, to):
-            return pltpu.make_async_remote_copy(
-                src_ref=source((me + d) % count),
-                dst_ref=target.at[to],
-                send_sem=ssem.at[stage, d],
-                recv_sem=rsem.at[stage, d],
-                device_id=device((me + d) % count),
-                device_id_type=MESH,
-            )
-
         def send():
-            for d in sorted(range(1, count), key=lambda d: -min(d, count - d)):
-                copy(d, me).start()
-
-        def arrive():
-            def one(d, carry):
-                copy(d, (me + count - d) % count).wait_recv()
-                return carry
-
-            lax.fori_loop(1, count, one, 0)
-
-        def leave():
-            def one(d, carry):
-                copy(d, me).wait_send()
-                return carry
-
-            lax.fori_loop(1, count, one, 0)
-
-        return send, arrive, leave
+            for d in far_first(count):
+                pltpu.make_async_remote_copy(
+                    src_ref=source((me + d) % count),
+                    dst_ref=target.at[me],
+                    send_sem=ssem.at[stage],
+                    recv_sem=rsem.at[stage],
+                    device_id=device((me + d) % count),
+                    device_id_type=MESH,
+                ).start()
+
+        others = target.at[pl.ds(0, count - 1)]
+        everything = pltpu.make_async_remote_copy(
+            src_ref=others, dst_ref=others, send_sem=ssem.at[stage], recv_sem=rsem.at[stage],
+            device_id=device((me + 1) % count), device_id_type=MESH,
+        )
+        return send, everything.wait_recv, everything.wait_send
 
     def to_sibling(i, source, target):
         return pltpu.make_async_remote_copy(
@@ -160,10 +143,6 @@
         src_ref=val.at[1], dst_ref=val.at[tiles + 1], send_sem=halo_send.at[1], recv_sem=halo_recv.at[1],
         device_id=(left, fld), device_id_type=MESH,
     )
-    pl.semaphore_wait(barrier, 3 + 2 * (ring - 1) + chips - 1)
-    to_right.start()
-    to_left.start()
-
     small[1].wait()
     small[2].wait()
     lane = lax.broadcasted_iota(I32, (FIELDS, TILE), 1)
@@ -204,9 +183,7 @@
     named = jnp.broadcast_to(named - 1.0, (rows, TILE))
     for g in range(ring):
         send0[g] = named[g * slots : (g + 1) * slots]
-    send, arrive0, leave0 = exchange(0, ring, first, on_first, lambda p: send0.at[p], recv0)
-    send()
-    recv0[first] = send0[first]
+    send_named, arrive0, leave0 = exchange(0, ring, first, on_first, lambda p: send0.at[p], recv0)
 
     small[4].wait()
     for r in range(4):
@@ -217,40 +194,52 @@
     ones = jnp.ones((FIELDS, TILE), F32)
     small[3].wait()
 
+    zeros = jnp.zeros((16, TILE), F32)
+
     def tile_sums(t):
         before, here, after = val[t], val[t + 1], val[t + 2]
         low = jnp.where(lane == 0, pltpu.roll(before, 1, 1), pltpu.roll(here, 1, 1))
         high = jnp.where(lane == TILE - 1, pltpu.roll(after, TILE - 1, 1), pltpu.roll(here, TILE - 1, 1))
         slope = 0.5 * (high - low)
+        operand, operator = [], []
         for k in range(reach):
-            rebuilt = here + cent[t, k : k + 1, :] * slope
-            operand = jnp.concatenate([rebuilt, ones], axis=0).astype(BF16)
-            sums = lax.dot_general(
-                operand, w[t, k], (((1,), (1,)), ((), ())), preferred_element_type=F32
-            )
+            rebuilt = jnp.concatenate([here + cent[t, k : k + 1, :] * slope, ones], axis=0)
+            operand.append(jnp.concatenate([zeros, rebuilt] if k % 2 else [rebuilt, zeros], axis=1))
+        for k in range(0, reach, 2):
+            operator.append(jnp.concatenate([w[t, k], w[t, k + 1]], axis=1))
+        product = lax.dot_general(
+            jnp.concatenate(operand, axis=0).astype(BF16), jnp.concatenate(operator, axis=0),
+            (((1,), (1,)), ((), ())), preferred_element_type=F32,
+        )
+        for k in range(reach):
+            sums = product[16 * k : 16 * k + 16, k // 2 * TILE : (k // 2 + 1) * TILE]
             area = sums[FIELDS : FIELDS + 1]
             code = jnp.round(sums[:FIELDS] * (LEVELS / jnp.maximum(area, LEAST)))
             part[pl.ds(k * PAD + t, FIELDS, stride=entries), :] = code
             part[pl.ds(FIELDS * entries + k * PAD + t, 1), :] = area
 
-    def chunk_sums(c):
+    def group_sums(c, carry):
         weights(c).wait()
-        for q in range(chunk):
-            tile_sums(c * chunk + q)
-
-    def inner(c, carry):
-        chunk_sums(c)
+        for q in range(4):
+            tile_sums(1 + 4 * c + q)
         return carry
 
-    lax.fori_loop(1, chunks - 1, inner, 0)
+    early = min(groups, 3)
+    lax.fori_loop(0, early, group_sums, 0)
+    pl.semaphore_wait(barrier, 3 + 2 * (ring - 1) + chips - 1)
+    to_right.start()
+    to_left.start()
+    send_named()
+    recv0[first] = send0[first]
+    lax.fori_loop(early, groups, group_sums, 0)
+    weights(groups).wait()
+    for q in range(rest):
+        tile_sums(1 + 4 * groups + q)
+    weights(groups + 1).wait()
     to_right.wait_recv()
     to_left.wait_recv()
-
-    def outer(c, carry):
-        chunk_sums(c * (chunks - 1))
-        return carry
-
-    lax.fori_loop(0, 2, outer, 0)
+    tile_sums(0)
+    tile_sums(tiles - 1)
 
     send, arrive1a, leave1a = exchange(1, ring, first, on_first, lambda p: send1a.at[p], recv1a)
     slotted = mixed(pick[...], part[FIELDS * entries :])
@@ -276,16 +265,16 @@
     member = member.astype(F32)
     gather = twice(member.T[: 8 * ring].astype(BF16))
     spread[...] = twice(member[:, : 8 * ring].astype(BF16))
-    all_ones = jnp.ones((16, reach * TILE), BF16)
 
     def column_area(c, carry):
         for q in range(chunk):
             t = c * chunk + q
-            area = jnp.dot(all_ones, w[t].reshape(reach * TILE, TILE), preferred_element_type=F32)
-            col_inverse[pl.ds(t, 1), :] = 1.0 / area[:1]
+            area = jnp.sum(w[t].reshape(reach * TILE, TILE).astype(F32), axis=0, keepdims=True)
+            col_inverse[pl.ds(t, 1), :] = 1.0 / area
         return carry
 
-    lax.fori_loop(0, chunks, column_area, 0)
+    chunk = 4 if tiles % 4 == 0 else 1
+    lax.fori_loop(0, tiles // chunk, column_area, 0)
 
     send, arrive2a, leave2a = exchange(3, ring, second, on_second, lambda p: send2a.at[p], recv2a)
     arrive1a()
@@ -340,13 +329,19 @@
     mine, other = pl.ds(2 * core, 2), pl.ds(2 - 2 * core, 2)
     pair_copy = to_sibling(0, send3.at[other], recv3)
     pair_copy.start()
-    for i, flux in enumerate((stress_u, stress_v, net_heat, freshwater)):
-        flux_out[i] = flux
     pair_copy.wait_recv()
     send3y[...] = send3[mine] + recv3[...]
     send, arrive, leave3 = exchange(5, chips, chip, on_chip, lambda p: send3y, recv3y)
     send()
     recv3y[chip] = send3y[...]
+    for i, flux in enumerate((stress_u, stress_v, net_heat, freshwater)):
+        for t in range(otiles):
+            flux_out[0, i : i + 1, t * TILE : (t + 1) * TILE] = flux[t : t + 1]
+    flux_copy = pltpu.make_async_copy(flux_out, flux_hbm, out_sem.at[0])
+    flux_copy.start()
+    for leave in (leave0, leave1a, leave1, leave2a, leave2, to_right.wait_send, to_left.wait_send):
+        leave()
+    pair_copy.wait_send()
     arrive()
     flux_sum = recv3y[0]
     for p in range(1, chips):
@@ -357,9 +352,10 @@
     send, arrive, leave4 = exchange(6, ring, second, on_second, lambda p: send4, recv4)
     send()
     recv4[second] = state
-    ocean_out[mine] = state
-    ocean_copy = to_sibling(1, ocean_out.at[mine], ocean_out.at[mine])
+    rows_next[mine] = state
+    ocean_copy = to_sibling(1, rows_next.at[mine], rows_next.at[mine])
     ocean_copy.start()
+    leave3()
     arrive()
 
     states = [recv4[:, r].reshape(ring * 8, TILE) for r in range(2)]
@@ -370,6 +366,15 @@
     send, arrive, leave5 = exchange(7, ring, first, on_first, lambda p: send5.at[p], recv5)
     send()
     recv5[first] = send5[first]
+    to_sibling(1, rows_next.at[mine], rows_next.at[other]).wait_recv()
+    for r in range(4):
+        for t in range(otiles):
+            ocean_out[r : r + 1, t * TILE : (t + 1) * TILE] = rows_next[r, t : t + 1]
+    next_copy = pltpu.make_async_copy(ocean_out, ocean_next_hbm, out_sem.at[1])
+    next_copy.start()
+    ocean_copy.wait_send()
+    leave4()
+    flux_copy.wait()
     arrive()
 
     states = [recv5[:, r].reshape(rows, TILE) for r in range(2)]
@@ -386,7 +391,7 @@
 
     def results(j):
         at = pl.ds(j * 8, 8)
-        return to_sibling(2 + j, atm_out.at[mine, at], atm_out.at[mine, at])
+        return to_sibling(2 + j, rows_back.at[mine, at], rows_back.at[mine, at])
 
     def remap(j, count):
         operand = lhs[j]
@@ -397,34 +402,40 @@
             two = jnp.where(row8 == q, sums[16:24] + sums[24:32], two)
         at = pl.ds(j * 8, 8)
         inverse = col_inverse[at]
-        atm_out[2 * core, at] = one * inverse
-        atm_out[2 * core + 1, at] = two * inverse
+        rows_back[2 * core, at] = one * inverse
+        rows_back[2 * core + 1, at] = two * inverse
         results(j).start()
 
     def full_remap(j, carry):
         remap(j, 8)
         return carry
 
-    whole, rest = tiles // 8, tiles % 8
+    whole, last = tiles // 8, tiles % 8
     lax.fori_loop(0, whole, full_remap, 0)
-    if rest:
-        remap(whole, rest)
-    blocks = whole + (rest > 0)
-
-    def finish(j, carry):
+    if last:
+        remap(whole, last)
+    leave5()
+    next_copy.wait()
+    for j in range(whole + (last > 0)):
         at = pl.ds(j * 8, 8)
-        to_sibling(2 + j, atm_out.at[mine, at], atm_out.at[other, at]).wait_recv()
+        to_sibling(2 + j, rows_back.at[mine, at], rows_back.at[other, at]).wait_recv()
+        for r in range(4):
+            for t in range(8 * j, min(8 * j + 8, tiles)):
+                atm_out[r : r + 1, t * TILE : (t + 1) * TILE] = rows_back[r, t : t + 1]
+    back_copy = pltpu.make_async_copy(atm_out, back_hbm, out_sem.at[2])
+    back_copy.start()
+    for j in range(whole + (last > 0)):
         results(j).wait_send()
-        return carry
-
-    lax.fori_loop(0, blocks, finish, 0)
-    to_sibling(1, ocean_out.at[mine], ocean_out.at[other]).wait_recv()
-    ocean_copy.wait_send()
-    pair_copy.wait_send()
-    to_right.wait_send()
-    to_left.wait_send()
-    for leave in (leave0, leave1a, leave1, leave2a, leave2, leave3, leave4, leave5):
-        leave()
+    back_copy.wait()
+
+
+def write_out(*refs):
+    sources, targets, sems = refs[:3], refs[3:6], refs[6]
+    copies = [pltpu.make_async_copy(s, t, sems.at[i]) for i, (s, t) in enumerate(zip(sources, targets))]
+    for copy in copies:
+        copy.start()
+    for copy in copies:
+        copy.wait()
 
 
 def shards(atm_state, owners, ocean_tile, centroid_offset, remap_weight, ocean_state):
@@ -439,19 +450,23 @@
     slots = MOST * ring
     rows = ring * slots
     entries = reach * PAD
-    most = max(ring, chips)
     hbm = pl.BlockSpec(memory_space=pltpu.HBM)
-    vmem = pl.BlockSpec(memory_space=pltpu.VMEM)
-    fluxes, ocean, back = pl.pallas_call(
+    out_shape = (
+        jax.ShapeDtypeStruct((1, 4, ocells), F32),
+        jax.ShapeDtypeStruct((4, ocells), F32),
+        jax.ShapeDtypeStruct((4, cells), F32),
+    )
+    results = pl.pallas_call(
         functools.partial(kernel, ring, samples, tiles, reach, otiles),
-        out_shape=(
-            jax.ShapeDtypeStruct((4, 8, TILE), F32),
-            jax.ShapeDtypeStruct((4, 8, TILE), F32),
-            jax.ShapeDtypeStruct((4, PAD, TILE), F32),
-        ),
+        out_shape=out_shape,
         in_specs=[hbm] * 6,
-        out_specs=(vmem, vmem, vmem),
+        out_specs=(hbm, hbm, hbm),
         scratch_shapes=[
+            pltpu.VMEM((1, 4, ocells), F32),
+            pltpu.VMEM((4, ocells), F32),
+            pltpu.VMEM((4, cells), F32),
+            pltpu.VMEM((4, 8, TILE), F32),
+            pltpu.VMEM((4, PAD, TILE), F32),
             pltpu.VMEM(atm_state.shape, BF16),
             pltpu.VMEM((reach, tiles), I32),
             pltpu.VMEM((reach, tiles), I32),
@@ -486,11 +501,12 @@
             pltpu.VMEM((ring, 2, slots, TILE), F32),
             pltpu.VMEM((ring, 2, slots, TILE), F32),
             pltpu.SemaphoreType.DMA((5,)),
+            pltpu.SemaphoreType.DMA((3,)),
             pltpu.SemaphoreType.DMA((tiles,)),
             pltpu.SemaphoreType.DMA((2,)),
             pltpu.SemaphoreType.DMA((2,)),
-            pltpu.SemaphoreType.DMA((8, most)),
-            pltpu.SemaphoreType.DMA((8, most)),
+            pltpu.SemaphoreType.DMA((8,)),
+            pltpu.SemaphoreType.DMA((8,)),
             pltpu.SemaphoreType.DMA((2 + PAD // 8,)),
             pltpu.SemaphoreType.DMA((2 + PAD // 8,)),
         ],
@@ -499,9 +515,15 @@
         ),
         name="coupling",
     )(atm_state, owners.T, ocean_tile.T, centroid_offset, remap_weight, ocean_state)
-    sample_fluxes = fluxes[:, :otiles].reshape(1, 4, ocells)
-    ocean_next = ocean[:, :otiles].reshape(4, ocells)
-    return sample_fluxes, ocean_next, back[:, :tiles].reshape(4, cells)
+    return pl.pallas_call(
+        write_out,
+        out_shape=out_shape,
+        in_specs=[hbm] * 3,
+        out_specs=(hbm, hbm, hbm),
+        scratch_shapes=[pltpu.SemaphoreType.DMA((3,))],
+        compiler_params=pltpu.CompilerParams(vmem_limit_bytes=60 * 1024 * 1024),
+        name="write_out",
+    )(*results)
 
 
 def solution(mesh):

time: 67.6 us -> 66.4 us (0.982)
  local copies, waits for them, and re-layouts: 4.16 us -> 0 us
  Pallas kernels: 62.4 us -> 65.6 us
    pallas_call x0 -> x1, Pallas kernels: none -> 3.74 us  [shards(): pl.pallas_call(write_out, out_shape=out_shape, in_specs=[hbm] * 3, out_sp...]
    unnamed x4 -> x0, local copies, waits for them, and re-layouts: 2.83 us -> none
    reshape x1 -> x0, local copies, waits for them, and re-layouts: 1.33 us -> none  [shards(): sample_fluxes = fluxes[:, :otiles].reshape(1, 4, ocells)]
where the time goes in v3:
time: 66.4 us; the launch traced here: 66.3 us
  Pallas kernels  65.6 us (99%)
    pallas_call x1, Pallas kernels, shards(): pl.pallas_call(functools.partial(kernel, ring, samples, tiles, reach, oti...  61.9 us
    pallas_call x1, Pallas kernels, shards(): pl.pallas_call(write_out, out_shape=out_shape, in_specs=[hbm] * 3, out_sp...  3.74 us

profile of v3, /device:TPU:1, one launch (start us, length us, event | category | flops | bytes accessed | tf_op | source)
XLA Modules:
  0.0 66.3 jit_solution(11622468166173164517)
XLA Ops:
  0.6 61.9 %coupling.1 = (f32[1,4,896]{2,1,0:T(4,128)}, f32[4,896]{1,0:T(4,128)}, f32[4,3584]{1,0:T(4,128)}) custom-call(bf16[1,8,3584]{2,1,0:T(8,128)(2,1)} %atm_hbm.1, s32[4,28]{1,0:T(4,128)} %bitcast.2, s32[4,28]{1,0:T(4,128)} %bitcast.3, f32[28,4,128]{2,1,0:T(4,128)} %cent_hbm.1, bf16[28,4,128,128]{3,2,1,0:T(8,128)(2,1)} %w_hbm.1, f32[4,896]{1,0:T(4,128)} %ocean_hbm.1), custom_call_target="tpu_custom_call" | custom-call | tf_op jit(solution)/shard_map/coupling/pallas_call | solution.py:459
  62.5 3.7 %write_out.1 = (f32[1,4,896]{2,1,0:T(4,128)}, f32[4,896]{1,0:T(4,128)}, f32[4,3584]{1,0:T(4,128)}) custom-call(f32[1,4,896]{2,1,0:T(4,128)} %get-tuple-element.6.refs_0_, f32[4,896]{1,0:T(4,128)} %get-tuple-element.7.refs_1_, f32[4,3584]{1,0:T(4,128)} %get-tuple-element.8.refs_2_), custom_call_target="tpu_custom_call" | custom-call | tf_op jit(solution)/shard_map/write_out/pallas_call | solution.py:518

commit v4 on v3

--- a/solution.py
+++ b/solution.py
@@ -14,6 +14,7 @@
 PAD = 32
 LEVELS = 5400.0
 LEAST = 1e-30
+PAIRS = (4, 6, 0, 2)
 MESH = pl.DeviceIdType.MESH
 F32 = jnp.float32
 BF16 = jnp.bfloat16
@@ -38,13 +39,12 @@
 def kernel(
     ring, samples, tiles, reach, otiles,
     atm_hbm, owners_hbm, otile_hbm, cent_hbm, w_hbm, ocean_hbm,
-    flux_hbm, ocean_next_hbm, back_hbm,
     flux_out, ocean_out, atm_out,
     rows_next, rows_back, atm, owners, otile, cent, w, ocean,
     val, part, pick, pick_t, spread, oc, table, col_inverse, lhs,
     send0, recv0, send1a, recv1a, send1, recv1, send2a, recv2a, send2, recv2,
     send3, recv3, send3y, recv3y, send4, recv4, send5, recv5,
-    in_sem, out_sem, w_sem, halo_send, halo_recv, ssem, rsem, psend, precv,
+    in_sem, w_sem, halo_send, halo_recv, ssem, rsem, psend, precv,
 ):
     cols = ring * ring
     chips = samples // 2
@@ -246,17 +246,19 @@
     for g in range(ring):
         send1a[g] = slotted[g * slots : (g + 1) * slots]
     send()
-    send, arrive1, leave1 = exchange(2, ring, first, on_first, lambda p: send1.at[p], recv1)
-    for f in range(0, FIELDS, 2):
+    recv1a[first] = send1a[first]
+    sent1 = []
+    for m, f in enumerate(PAIRS):
         one = mixed(pick[...], part[f * entries : (f + 1) * entries])
         two = mixed(pick[...], part[(f + 1) * entries : (f + 2) * entries])
         for g in range(ring):
             at = slice(g * slots, (g + 1) * slots)
             pair = jnp.concatenate([one[at], two[at]], axis=0)
-            send1[g, f * slots : (f + 2) * slots] = pair.astype(I32).astype(I16)
-    send()
-    recv1a[first] = send1a[first]
-    recv1[first] = send1[first]
+            send1[m, g] = pair.astype(I32).astype(I16)
+        send, *ends = exchange(2 + m, ring, first, on_first, lambda p: send1.at[m, p], recv1.at[m])
+        send()
+        sent1.append(ends)
+        recv1[m, first] = send1[m, first]
 
     arrive0()
     row = lax.broadcasted_iota(I32, (rows, TILE), 0)
@@ -276,34 +278,44 @@
     chunk = 4 if tiles % 4 == 0 else 1
     lax.fori_loop(0, tiles // chunk, column_area, 0)
 
-    send, arrive2a, leave2a = exchange(3, ring, second, on_second, lambda p: send2a.at[p], recv2a)
+    send, arrive2a, leave2a = exchange(6, ring, second, on_second, lambda p: send2a.at[p], recv2a)
     arrive1a()
     areas = recv1a[...].reshape(rows, TILE)
     dense_area = mixed(gather, areas)
     send2a[...] = dense_area.reshape(ring, 8, TILE)
     send()
+    recv2a[second] = send2a[second]
     per_area = 1.0 / jnp.maximum(dense_area, LEAST)
-    send, arrive2, leave2 = exchange(4, ring, second, on_second, lambda p: send2.at[p], recv2)
-    arrive1()
-    for f in range(0, FIELDS, 2):
-        pair = recv1[:, f * slots : (f + 2) * slots].astype(I32).astype(F32)
+    sent2 = []
+    for m in range(len(PAIRS)):
+        arrive, _ = sent1[m]
+        arrive()
+        pair = recv1[m].astype(I32).astype(F32)
         one = mixed(gather, pair[:, :slots].reshape(rows, TILE) * areas) * per_area
         two = mixed(gather, pair[:, slots:].reshape(rows, TILE) * areas) * per_area
         both = jnp.concatenate([one.reshape(ring, 8, TILE), two.reshape(ring, 8, TILE)], axis=1)
-        send2[:, f * 8 : (f + 2) * 8] = jnp.round(both).astype(I32).astype(I16)
-    send()
-    recv2a[second] = send2a[second]
-    recv2[second] = send2[second]
+        send2[m] = jnp.round(both).astype(I32).astype(I16)
+        send, *ends = exchange(7 + m, ring, second, on_second, lambda p: send2.at[m, p], recv2.at[m])
+        send()
+        sent2.append(ends)
+        recv2[m, second] = send2[m, second]
+
     arrive2a()
-    arrive2()
-
     coverage = jnp.zeros((8, TILE), F32)
-    total = jnp.zeros((FIELDS, 8, TILE), F32)
     for p in range(ring):
-        area = recv2a[p]
-        coverage = coverage + area
-        total = total + recv2[p].astype(I32).astype(F32).reshape(FIELDS, 8, TILE) * area[None]
-    forcing = total * (1.0 / (LEVELS * jnp.maximum(coverage, 1.0)))[None]
+        coverage = coverage + recv2a[p]
+    per_coverage = 1.0 / (LEVELS * jnp.maximum(coverage, 1.0))
+    forcing = [None] * FIELDS
+    for m, f in enumerate(PAIRS):
+        arrive, _ = sent2[m]
+        arrive()
+        one = two = jnp.zeros((8, TILE), F32)
+        for p in range(ring):
+            pair = recv2[m, p].astype(I32).astype(F32)
+            one = one + pair[:8] * recv2a[p]
+            two = two + pair[8:] * recv2a[p]
+        forcing[f] = one * per_coverage
+        forcing[f + 1] = two * per_coverage
 
     sst, uo, vo = oc[0], oc[1], oc[2]
     slip_u = forcing[0] - uo
@@ -331,15 +343,15 @@
     pair_copy.start()
     pair_copy.wait_recv()
     send3y[...] = send3[mine] + recv3[...]
-    send, arrive, leave3 = exchange(5, chips, chip, on_chip, lambda p: send3y, recv3y)
+    send, arrive, leave3 = exchange(11, chips, chip, on_chip, lambda p: send3y, recv3y)
     send()
     recv3y[chip] = send3y[...]
     for i, flux in enumerate((stress_u, stress_v, net_heat, freshwater)):
         for t in range(otiles):
             flux_out[0, i : i + 1, t * TILE : (t + 1) * TILE] = flux[t : t + 1]
-    flux_copy = pltpu.make_async_copy(flux_out, flux_hbm, out_sem.at[0])
-    flux_copy.start()
-    for leave in (leave0, leave1a, leave1, leave2a, leave2, to_right.wait_send, to_left.wait_send):
+    for leave in (leave0, leave1a, leave2a, to_right.wait_send, to_left.wait_send):
+        leave()
+    for _, leave in sent1 + sent2:
         leave()
     pair_copy.wait_send()
     arrive()
@@ -349,7 +361,7 @@
     state = oc[mine] + (0.5 / samples) * flux_sum
     send4[...] = state
 
-    send, arrive, leave4 = exchange(6, ring, second, on_second, lambda p: send4, recv4)
+    send, arrive, leave4 = exchange(12, ring, second, on_second, lambda p: send4, recv4)
     send()
     recv4[second] = state
     rows_next[mine] = state
@@ -363,18 +375,15 @@
     for p in range(ring):
         for r in range(2):
             send5[p, r] = slotted[p * slots : (p + 1) * slots, r * TILE : (r + 1) * TILE]
-    send, arrive, leave5 = exchange(7, ring, first, on_first, lambda p: send5.at[p], recv5)
+    send, arrive, leave5 = exchange(13, ring, first, on_first, lambda p: send5.at[p], recv5)
     send()
     recv5[first] = send5[first]
     to_sibling(1, rows_next.at[mine], rows_next.at[other]).wait_recv()
     for r in range(4):
         for t in range(otiles):
             ocean_out[r : r + 1, t * TILE : (t + 1) * TILE] = rows_next[r, t : t + 1]
-    next_copy = pltpu.make_async_copy(ocean_out, ocean_next_hbm, out_sem.at[1])
-    next_copy.start()
     ocean_copy.wait_send()
     leave4()
-    flux_copy.wait()
     arrive()
 
     states = [recv5[:, r].reshape(rows, TILE) for r in range(2)]
@@ -415,27 +424,14 @@
     if last:
         remap(whole, last)
     leave5()
-    next_copy.wait()
     for j in range(whole + (last > 0)):
         at = pl.ds(j * 8, 8)
         to_sibling(2 + j, rows_back.at[mine, at], rows_back.at[other, at]).wait_recv()
         for r in range(4):
             for t in range(8 * j, min(8 * j + 8, tiles)):
                 atm_out[r : r + 1, t * TILE : (t + 1) * TILE] = rows_back[r, t : t + 1]
-    back_copy = pltpu.make_async_copy(atm_out, back_hbm, out_sem.at[2])
-    back_copy.start()
     for j in range(whole + (last > 0)):
         results(j).wait_send()
-    back_copy.wait()
-
-
-def write_out(*refs):
-    sources, targets, sems = refs[:3], refs[3:6], refs[6]
-    copies = [pltpu.make_async_copy(s, t, sems.at[i]) for i, (s, t) in enumerate(zip(sources, targets))]
-    for copy in copies:
-        copy.start()
-    for copy in copies:
-        copy.wait()
 
 
 def shards(atm_state, owners, ocean_tile, centroid_offset, remap_weight, ocean_state):
@@ -451,6 +447,7 @@
     rows = ring * slots
     entries = reach * PAD
     hbm = pl.BlockSpec(memory_space=pltpu.HBM)
+    vmem = pl.BlockSpec(memory_space=pltpu.VMEM)
     out_shape = (
         jax.ShapeDtypeStruct((1, 4, ocells), F32),
         jax.ShapeDtypeStruct((4, ocells), F32),
@@ -458,13 +455,10 @@
     )
     results = pl.pallas_call(
         functools.partial(kernel, ring, samples, tiles, reach, otiles),
-        out_shape=out_shape,
+        out_shape=tuple(pltpu.VMEM(s.shape, s.dtype) for s in out_shape),
         in_specs=[hbm] * 6,
-        out_specs=(hbm, hbm, hbm),
+        out_specs=(vmem, vmem, vmem),
         scratch_shapes=[
-            pltpu.VMEM((1, 4, ocells), F32),
-            pltpu.VMEM((4, ocells), F32),
-            pltpu.VMEM((4, cells), F32),
             pltpu.VMEM((4, 8, TILE), F32),
             pltpu.VMEM((4, PAD, TILE), F32),
             pltpu.VMEM(atm_state.shape, BF16),
@@ -486,12 +480,12 @@
             pltpu.VMEM((ring, slots, TILE), F32),
             pltpu.VMEM((ring, slots, TILE), F32),
             pltpu.VMEM((ring, slots, TILE), F32),
-            pltpu.VMEM((ring, FIELDS * slots, TILE), I16),
-            pltpu.VMEM((ring, FIELDS * slots, TILE), I16),
+            pltpu.VMEM((len(PAIRS), ring, 2 * slots, TILE), I16),
+            pltpu.VMEM((len(PAIRS), ring, 2 * slots, TILE), I16),
             pltpu.VMEM((ring, 8, TILE), F32),
             pltpu.VMEM((ring, 8, TILE), F32),
-            pltpu.VMEM((ring, FIELDS * 8, TILE), I16),
-            pltpu.VMEM((ring, FIELDS * 8, TILE), I16),
+            pltpu.VMEM((len(PAIRS), ring, 16, TILE), I16),
+            pltpu.VMEM((len(PAIRS), ring, 16, TILE), I16),
             pltpu.VMEM((4, 8, TILE), F32),
             pltpu.VMEM((2, 8, TILE), F32),
             pltpu.VMEM((2, 8, TILE), F32),
@@ -501,12 +495,11 @@
             pltpu.VMEM((ring, 2, slots, TILE), F32),
             pltpu.VMEM((ring, 2, slots, TILE), F32),
             pltpu.SemaphoreType.DMA((5,)),
-            pltpu.SemaphoreType.DMA((3,)),
             pltpu.SemaphoreType.DMA((tiles,)),
             pltpu.SemaphoreType.DMA((2,)),
             pltpu.SemaphoreType.DMA((2,)),
-            pltpu.SemaphoreType.DMA((8,)),
-            pltpu.SemaphoreType.DMA((8,)),
+            pltpu.SemaphoreType.DMA((14,)),
+            pltpu.SemaphoreType.DMA((14,)),
             pltpu.SemaphoreType.DMA((2 + PAD // 8,)),
             pltpu.SemaphoreType.DMA((2 + PAD // 8,)),
         ],
@@ -515,15 +508,7 @@
         ),
         name="coupling",
     )(atm_state, owners.T, ocean_tile.T, centroid_offset, remap_weight, ocean_state)
-    return pl.pallas_call(
-        write_out,
-        out_shape=out_shape,
-        in_specs=[hbm] * 3,
-        out_specs=(hbm, hbm, hbm),
-        scratch_shapes=[pltpu.SemaphoreType.DMA((3,))],
-        compiler_params=pltpu.CompilerParams(vmem_limit_bytes=60 * 1024 * 1024),
-        name="write_out",
-    )(*results)
+    return results
 
 
 def solution(mesh):

time: 66.4 us -> 64.6 us (0.973)
  Pallas kernels: 65.6 us -> 62 us
  local copies, waits for them, and re-layouts: 0 us -> 1.82 us
    pallas_call x1 -> x0, Pallas kernels: 3.74 us -> none  [shards(): pl.pallas_call(write_out, out_shape=out_shape, in_specs=[hbm] * 3, out_sp...]
    unnamed x0 -> x3, local copies, waits for them, and re-layouts: none -> 1.82 us
where the time goes in v4:
time: 64.6 us; the launch traced here: 64.5 us
  Pallas kernels  62 us (96%)
  local copies, waits for them, and re-layouts  1.82 us (3%)
    pallas_call x1, Pallas kernels, shards(): pl.pallas_call(functools.partial(kernel, ring, samples, tiles, reach, oti...  62 us
    unnamed x3, local copies, waits for them, and re-layouts  1.82 us

profile of v4, /device:TPU:1, one launch (start us, length us, event | category | flops | bytes accessed | tf_op | source)
XLA Modules:
  0.0 64.5 jit_solution(17845024999053812231)
XLA Ops:
  0.6 62.0 %coupling.1 = (f32[1,4,896]{2,1,0:T(4,128)S(1)}, f32[4,896]{1,0:T(4,128)S(1)}, f32[4,3584]{1,0:T(4,128)S(1)}) custom-call(bf16[1,8,3584]{2,1,0:T(8,128)(2,1)} %atm_hbm.1, s32[4,28]{1,0:T(4,128)} %bitcast.2, s32[4,28]{1,0:T(4,128)} %bitcast.3, f32[28,4,128]{2,1,0:T(4,128)} %cent_hbm.1, bf16[28,4,128,128]{3,2,1,0:T(8,128)(2,1)} %w_hbm.1, f32[4,896]{1,0:T(4,128)} %ocean_hbm.1), custom_call_target="tpu_custom_call" | custom-call | tf_op jit(solution)/shard_map/coupling/pallas_call | solution.py:456
  62.7 0.6 copy.12
  63.3 0.6 copy.13
  63.9 0.6 copy.14

commit v5 on v4

--- a/solution.py
+++ b/solution.py
@@ -14,7 +14,6 @@
 PAD = 32
 LEVELS = 5400.0
 LEAST = 1e-30
-PAIRS = (4, 6, 0, 2)
 MESH = pl.DeviceIdType.MESH
 F32 = jnp.float32
 BF16 = jnp.bfloat16
@@ -42,7 +41,7 @@
     flux_out, ocean_out, atm_out,
     rows_next, rows_back, atm, owners, otile, cent, w, ocean,
     val, part, pick, pick_t, spread, oc, table, col_inverse, lhs,
-    send0, recv0, send1a, recv1a, send1, recv1, send2a, recv2a, send2, recv2,
+    send0, recv0, ends_sent, ends_got, send1a, recv1a, send1, recv1, send2a, recv2a, send2, recv2,
     send3, recv3, send3y, recv3y, send4, recv4, send5, recv5,
     in_sem, w_sem, halo_send, halo_recv, ssem, rsem, psend, precv,
 ):
@@ -51,6 +50,7 @@
     slots = MOST * ring
     rows = ring * slots
     entries = reach * PAD
+    ends = 2 * reach
     col = lax.axis_index("cols")
     fld = lax.axis_index("fld")
     x, z = col // ring, col % ring
@@ -102,7 +102,7 @@
         at = pl.ds(*spans[c]) if isinstance(c, int) else pl.ds(1 + 4 * c, 4)
         return pltpu.make_async_copy(w_hbm.at[at], w.at[at], w_sem.at[c])
 
-    for c in range(groups + 2):
+    for c in (groups + 1, groups, *range(groups)):
         weights(c).start()
 
     def exchange(stage, count, me, device, source, target):
@@ -173,6 +173,18 @@
         place = (1 - core) * low + core * high
         return jnp.where(owner < cols, group * slots + rank * ring + place, -1)
 
+    tile_down = jnp.broadcast_to(tile_across, (entries, entries)).T
+
+    def end_rows(x):
+        at = [k * PAD for k in range(reach)] + [k * PAD + tiles - 1 for k in range(reach)]
+        return jnp.concatenate([x[i : i + 1] for i in at], axis=0)
+
+    end_owner = end_rows(owner_down).astype(I32)
+    end_high = end_owner // ring
+    end_low = end_owner - end_high * ring
+    end_group = (1 - core) * end_high + core * end_low
+    end_row = ((1 - core) * end_low + core * end_high) * 8 + end_rows(tile_down).astype(I32)
+
     slot_across = slot(owner_across, rank_across)
     slot_down = slot(owner_down[:, :1], rank_down)
     pick_f = (lax.broadcasted_iota(I32, (rows, entries), 0) == slot_across).astype(F32)
@@ -182,7 +194,8 @@
     named = jnp.sum(pick_f * (tile_across + 1.0), axis=1, keepdims=True)
     named = jnp.broadcast_to(named - 1.0, (rows, TILE))
     for g in range(ring):
-        send0[g] = named[g * slots : (g + 1) * slots]
+        send0[g, :slots] = named[g * slots : (g + 1) * slots]
+        send0[g, slots : slots + ends] = jnp.where(end_group == g, end_row, -1).astype(F32)
     send_named, arrive0, leave0 = exchange(0, ring, first, on_first, lambda p: send0.at[p], recv0)
 
     small[4].wait()
@@ -191,20 +204,24 @@
         for t in range(otiles):
             oc[r, t : t + 1, :] = ocean[r : r + 1, t * TILE : (t + 1) * TILE]
 
-    ones = jnp.ones((FIELDS, TILE), F32)
     small[3].wait()
-
     zeros = jnp.zeros((16, TILE), F32)
-
-    def tile_sums(t):
-        before, here, after = val[t], val[t + 1], val[t + 2]
+    row8 = lax.broadcasted_iota(I32, (8, TILE), 0)
+    last_lane = TILE - 1
+    extra = jnp.where(row8 == 0, 1.0, 0.0)
+    extra = jnp.where((row8 == 1) & (lane == 0) | (row8 == 2) & (lane == last_lane), 1.0, extra)
+
+    def rebuild(t, before, here, after):
         low = jnp.where(lane == 0, pltpu.roll(before, 1, 1), pltpu.roll(here, 1, 1))
-        high = jnp.where(lane == TILE - 1, pltpu.roll(after, TILE - 1, 1), pltpu.roll(here, TILE - 1, 1))
+        high = jnp.where(lane == last_lane, pltpu.roll(after, last_lane, 1), pltpu.roll(here, last_lane, 1))
         slope = 0.5 * (high - low)
+        return [here + cent[t, k : k + 1, :] * slope for k in range(reach)]
+
+    def tile_sums(t, rebuilt):
         operand, operator = [], []
         for k in range(reach):
-            rebuilt = jnp.concatenate([here + cent[t, k : k + 1, :] * slope, ones], axis=0)
-            operand.append(jnp.concatenate([zeros, rebuilt] if k % 2 else [rebuilt, zeros], axis=1))
+            block = jnp.concatenate([rebuilt[k], extra], axis=0)
+            operand.append(jnp.concatenate([zeros, block] if k % 2 else [block, zeros], axis=1))
         for k in range(0, reach, 2):
             operator.append(jnp.concatenate([w[t, k], w[t, k + 1]], axis=1))
         product = lax.dot_general(
@@ -217,56 +234,85 @@
             code = jnp.round(sums[:FIELDS] * (LEVELS / jnp.maximum(area, LEAST)))
             part[pl.ds(k * PAD + t, FIELDS, stride=entries), :] = code
             part[pl.ds(FIELDS * entries + k * PAD + t, 1), :] = area
+        return [product[16 * k : 16 * k + 16, k // 2 * TILE : (k // 2 + 1) * TILE] for k in range(reach)]
+
+    def inner_sums(t):
+        return tile_sums(t, rebuild(t, val[t], val[t + 1], val[t + 2]))
 
     def group_sums(c, carry):
         weights(c).wait()
         for q in range(4):
-            tile_sums(1 + 4 * c + q)
+            inner_sums(1 + 4 * c + q)
         return carry
+
+    weights(groups + 1).wait()
+    here = val[1]
+    cut = [jnp.where(lane == 0, 0.0, x) for x in rebuild(0, here, here, val[2])]
+    low_weights = [x[FIELDS + 1 : FIELDS + 2] for x in tile_sums(0, cut)]
+    weights(groups).wait()
+    here = val[tiles]
+    cut = [jnp.where(lane == last_lane, 0.0, x) for x in rebuild(tiles - 1, val[tiles - 1], here, here)]
+    high_weights = [x[FIELDS + 2 : FIELDS + 3] for x in tile_sums(tiles - 1, cut)]
+    end_weights = jnp.concatenate(low_weights + high_weights, axis=0)
+    for g in range(ring):
+        send0[g, slots + ends :] = end_weights
+    for q in range(rest):
+        inner_sums(1 + 4 * groups + q)
 
     early = min(groups, 3)
     lax.fori_loop(0, early, group_sums, 0)
     pl.semaphore_wait(barrier, 3 + 2 * (ring - 1) + chips - 1)
+    send_named()
     to_right.start()
     to_left.start()
-    send_named()
     recv0[first] = send0[first]
     lax.fori_loop(early, groups, group_sums, 0)
-    weights(groups).wait()
-    for q in range(rest):
-        tile_sums(1 + 4 * groups + q)
-    weights(groups + 1).wait()
-    to_right.wait_recv()
-    to_left.wait_recv()
-    tile_sums(0)
-    tile_sums(tiles - 1)
 
     send, arrive1a, leave1a = exchange(1, ring, first, on_first, lambda p: send1a.at[p], recv1a)
     slotted = mixed(pick[...], part[FIELDS * entries :])
     for g in range(ring):
         send1a[g] = slotted[g * slots : (g + 1) * slots]
     send()
+    sent1 = []
+    for m in range(2):
+        codes = []
+        for f in range(4 * m, 4 * m + 4):
+            codes.append(mixed(pick[...], part[f * entries : (f + 1) * entries]))
+        for g in range(ring):
+            block = jnp.concatenate([x[g * slots : (g + 1) * slots] for x in codes], axis=0)
+            send1[m, g] = block.astype(I32).astype(I16)
+        send, *done = exchange(2 + m, ring, first, on_first, lambda p: send1.at[m, p], recv1.at[m])
+        send()
+        sent1.append(done)
     recv1a[first] = send1a[first]
-    sent1 = []
-    for m, f in enumerate(PAIRS):
-        one = mixed(pick[...], part[f * entries : (f + 1) * entries])
-        two = mixed(pick[...], part[(f + 1) * entries : (f + 2) * entries])
-        for g in range(ring):
-            at = slice(g * slots, (g + 1) * slots)
-            pair = jnp.concatenate([one[at], two[at]], axis=0)
-            send1[m, g] = pair.astype(I32).astype(I16)
-        send, *ends = exchange(2 + m, ring, first, on_first, lambda p: send1.at[m, p], recv1.at[m])
-        send()
-        sent1.append(ends)
+    for m in range(2):
         recv1[m, first] = send1[m, first]
+
+    to_right.wait_recv()
+    to_left.wait_recv()
+    end_values = jnp.zeros((8, TILE), F32)
+    low = rebuild(0, val[0], val[1], val[2])
+    high = rebuild(tiles - 1, val[tiles - 1], val[tiles], val[tiles + 1])
+    for k in range(reach):
+        moved = pltpu.roll(low[k], k, 1) if k else low[k]
+        end_values = jnp.where(lane == k, moved, end_values)
+        end_values = jnp.where(lane == reach + k, pltpu.roll(high[k], reach + 1 + k, 1), end_values)
+    end_values = end_values.astype(BF16).astype(F32)
+    ends_sent[...] = jnp.concatenate([end_values, jnp.zeros((TILE - 8, TILE), F32)], axis=0).T[:ends]
+    send, arrive_ends, leave_ends = exchange(4, ring, first, on_first, lambda p: ends_sent, ends_got)
+    send()
+    ends_got[first] = ends_sent[...]
 
     arrive0()
     row = lax.broadcasted_iota(I32, (rows, TILE), 0)
-    target = recv0[...].reshape(rows, TILE).astype(I32)
-    member = (target >= 0) & (target + 8 * (row % ring) == lax.broadcasted_iota(I32, (rows, TILE), 1))
-    member = member.astype(F32)
-    gather = twice(member.T[: 8 * ring].astype(BF16))
+    lane_of = lax.broadcasted_iota(I32, (rows, TILE), 1)
+    target = recv0[:, :slots].reshape(rows, TILE).astype(I32)
+    member = ((target >= 0) & (target + 8 * (row % ring) == lane_of)).astype(F32)
     spread[...] = twice(member[:, : 8 * ring].astype(BF16))
+    target = recv0[:, slots : slots + ends].reshape(ring * ends, TILE).astype(I32)
+    member_ends = (target == lax.broadcasted_iota(I32, (ring * ends, TILE), 1)).astype(F32)
+    gather = twice(jnp.concatenate([member, member_ends], axis=0).T[: 8 * ring].astype(BF16))
+    end_weights = recv0[:, slots + ends :].reshape(ring * ends, TILE) * LEVELS
 
     def column_area(c, carry):
         for q in range(chunk):
@@ -278,44 +324,41 @@
     chunk = 4 if tiles % 4 == 0 else 1
     lax.fori_loop(0, tiles // chunk, column_area, 0)
 
-    send, arrive2a, leave2a = exchange(6, ring, second, on_second, lambda p: send2a.at[p], recv2a)
+    send, arrive2a, leave2a = exchange(5, ring, second, on_second, lambda p: send2a.at[p], recv2a)
     arrive1a()
     areas = recv1a[...].reshape(rows, TILE)
-    dense_area = mixed(gather, areas)
+    dense_area = mixed(gather, jnp.concatenate([areas, jnp.zeros((ring * ends, TILE), F32)], axis=0))
     send2a[...] = dense_area.reshape(ring, 8, TILE)
     send()
     recv2a[second] = send2a[second]
     per_area = 1.0 / jnp.maximum(dense_area, LEAST)
-    sent2 = []
-    for m in range(len(PAIRS)):
+    send, arrive2, leave2 = exchange(6, ring, second, on_second, lambda p: send2.at[p], recv2)
+    arrive_ends()
+    end_values = ends_got[...].reshape(ring * ends, TILE)
+    for m in range(2):
         arrive, _ = sent1[m]
         arrive()
-        pair = recv1[m].astype(I32).astype(F32)
-        one = mixed(gather, pair[:, :slots].reshape(rows, TILE) * areas) * per_area
-        two = mixed(gather, pair[:, slots:].reshape(rows, TILE) * areas) * per_area
-        both = jnp.concatenate([one.reshape(ring, 8, TILE), two.reshape(ring, 8, TILE)], axis=1)
-        send2[m] = jnp.round(both).astype(I32).astype(I16)
-        send, *ends = exchange(7 + m, ring, second, on_second, lambda p: send2.at[m, p], recv2.at[m])
-        send()
-        sent2.append(ends)
-        recv2[m, second] = send2[m, second]
-
+        block = recv1[m].astype(I32).astype(F32)
+        means = []
+        for i in range(4):
+            f = 4 * m + i
+            sums = block[:, i * slots : (i + 1) * slots].reshape(rows, TILE) * areas
+            sums = jnp.concatenate([sums, end_values[:, f : f + 1] * end_weights], axis=0)
+            means.append((mixed(gather, sums) * per_area).reshape(ring, 8, TILE))
+        block = jnp.concatenate(means, axis=1)
+        send2[:, 32 * m : 32 * m + 32] = jnp.round(block).astype(I32).astype(I16)
+    send()
+    recv2[second] = send2[second]
     arrive2a()
+    arrive2()
+
     coverage = jnp.zeros((8, TILE), F32)
+    total = jnp.zeros((FIELDS, 8, TILE), F32)
     for p in range(ring):
-        coverage = coverage + recv2a[p]
-    per_coverage = 1.0 / (LEVELS * jnp.maximum(coverage, 1.0))
-    forcing = [None] * FIELDS
-    for m, f in enumerate(PAIRS):
-        arrive, _ = sent2[m]
-        arrive()
-        one = two = jnp.zeros((8, TILE), F32)
-        for p in range(ring):
-            pair = recv2[m, p].astype(I32).astype(F32)
-            one = one + pair[:8] * recv2a[p]
-            two = two + pair[8:] * recv2a[p]
-        forcing[f] = one * per_coverage
-        forcing[f + 1] = two * per_coverage
+        area = recv2a[p]
+        coverage = coverage + area
+        total = total + recv2[p].astype(I32).astype(F32).reshape(FIELDS, 8, TILE) * area[None]
+    forcing = total * (1.0 / (LEVELS * jnp.maximum(coverage, 1.0)))[None]
 
     sst, uo, vo = oc[0], oc[1], oc[2]
     slip_u = forcing[0] - uo
@@ -343,15 +386,15 @@
     pair_copy.start()
     pair_copy.wait_recv()
     send3y[...] = send3[mine] + recv3[...]
-    send, arrive, leave3 = exchange(11, chips, chip, on_chip, lambda p: send3y, recv3y)
+    send, arrive, leave3 = exchange(7, chips, chip, on_chip, lambda p: send3y, recv3y)
     send()
     recv3y[chip] = send3y[...]
     for i, flux in enumerate((stress_u, stress_v, net_heat, freshwater)):
         for t in range(otiles):
             flux_out[0, i : i + 1, t * TILE : (t + 1) * TILE] = flux[t : t + 1]
-    for leave in (leave0, leave1a, leave2a, to_right.wait_send, to_left.wait_send):
+    for leave in (leave0, leave1a, leave_ends, leave2a, leave2, to_right.wait_send, to_left.wait_send):
         leave()
-    for _, leave in sent1 + sent2:
+    for _, leave in sent1:
         leave()
     pair_copy.wait_send()
     arrive()
@@ -361,7 +404,7 @@
     state = oc[mine] + (0.5 / samples) * flux_sum
     send4[...] = state
 
-    send, arrive, leave4 = exchange(12, ring, second, on_second, lambda p: send4, recv4)
+    send, arrive, leave4 = exchange(8, ring, second, on_second, lambda p: send4, recv4)
     send()
     recv4[second] = state
     rows_next[mine] = state
@@ -375,7 +418,7 @@
     for p in range(ring):
         for r in range(2):
             send5[p, r] = slotted[p * slots : (p + 1) * slots, r * TILE : (r + 1) * TILE]
-    send, arrive, leave5 = exchange(13, ring, first, on_first, lambda p: send5.at[p], recv5)
+    send, arrive, leave5 = exchange(9, ring, first, on_first, lambda p: send5.at[p], recv5)
     send()
     recv5[first] = send5[first]
     to_sibling(1, rows_next.at[mine], rows_next.at[other]).wait_recv()
@@ -396,7 +439,6 @@
             block = [high[at, :TILE], low[at, :TILE], high[at, TILE:], low[at, TILE:]]
             lhs[j, :, k * TILE : (k + 1) * TILE] = jnp.concatenate(block, axis=0).astype(BF16)
 
-    row8 = lax.broadcasted_iota(I32, (8, TILE), 0)
 
     def results(j):
         at = pl.ds(j * 8, 8)
@@ -476,16 +518,18 @@
             pltpu.VMEM((8, TILE), F32),
             pltpu.VMEM((PAD, TILE), F32),
             pltpu.VMEM((PAD // 8, 32, reach * TILE), BF16),
+            pltpu.VMEM((ring, slots + 4 * reach, TILE), F32),
+            pltpu.VMEM((ring, slots + 4 * reach, TILE), F32),
+            pltpu.VMEM((2 * reach, TILE), F32),
+            pltpu.VMEM((ring, 2 * reach, TILE), F32),
             pltpu.VMEM((ring, slots, TILE), F32),
             pltpu.VMEM((ring, slots, TILE), F32),
-            pltpu.VMEM((ring, slots, TILE), F32),
-            pltpu.VMEM((ring, slots, TILE), F32),
-            pltpu.VMEM((len(PAIRS), ring, 2 * slots, TILE), I16),
-            pltpu.VMEM((len(PAIRS), ring, 2 * slots, TILE), I16),
+            pltpu.VMEM((2, ring, 4 * slots, TILE), I16),
+            pltpu.VMEM((2, ring, 4 * slots, TILE), I16),
             pltpu.VMEM((ring, 8, TILE), F32),
             pltpu.VMEM((ring, 8, TILE), F32),
-            pltpu.VMEM((len(PAIRS), ring, 16, TILE), I16),
-            pltpu.VMEM((len(PAIRS), ring, 16, TILE), I16),
+            pltpu.VMEM((ring, FIELDS * 8, TILE), I16),
+            pltpu.VMEM((ring, FIELDS * 8, TILE), I16),
             pltpu.VMEM((4, 8, TILE), F32),
             pltpu.VMEM((2, 8, TILE), F32),
             pltpu.VMEM((2, 8, TILE), F32),
@@ -498,8 +542,8 @@
             pltpu.SemaphoreType.DMA((tiles,)),
             pltpu.SemaphoreType.DMA((2,)),
             pltpu.SemaphoreType.DMA((2,)),
-            pltpu.SemaphoreType.DMA((14,)),
-            pltpu.SemaphoreType.DMA((14,)),
+            pltpu.SemaphoreType.DMA((10,)),
+            pltpu.SemaphoreType.DMA((10,)),
             pltpu.SemaphoreType.DMA((2 + PAD // 8,)),
             pltpu.SemaphoreType.DMA((2 + PAD // 8,)),
         ],

time: 64.6 us -> 61.6 us (0.954)
  Pallas kernels: 62 us -> 59 us
    pallas_call x1, Pallas kernels: 62 us -> 59 us  [shards(): pl.pallas_call(functools.partial(kernel, ring, samples, tiles, reach, oti...]
where the time goes in v5:
time: 61.6 us; the launch traced here: 61.5 us
  Pallas kernels  59 us (96%)
  local copies, waits for them, and re-layouts  1.82 us (3%)
  between operations  0.64 us (1%)
    pallas_call x1, Pallas kernels, shards(): pl.pallas_call(functools.partial(kernel, ring, samples, tiles, reach, oti...  59 us
    unnamed x3, local copies, waits for them, and re-layouts  1.82 us

profile of v5, /device:TPU:1, one launch (start us, length us, event | category | flops | bytes accessed | tf_op | source)
XLA Modules:
  0.0 61.5 jit_solution(4963337627858684887)
XLA Ops:
  0.6 59.0 %coupling.1 = (f32[1,4,896]{2,1,0:T(4,128)S(1)}, f32[4,896]{1,0:T(4,128)S(1)}, f32[4,3584]{1,0:T(4,128)S(1)}) custom-call(bf16[1,8,3584]{2,1,0:T(8,128)(2,1)} %atm_hbm.1, s32[4,28]{1,0:T(4,128)} %bitcast.2, s32[4,28]{1,0:T(4,128)} %bitcast.3, f32[28,4,128]{2,1,0:T(4,128)} %cent_hbm.1, bf16[28,4,128,128]{3,2,1,0:T(8,128)(2,1)} %w_hbm.1, f32[4,896]{1,0:T(4,128)} %ocean_hbm.1), custom_call_target="tpu_custom_call" | custom-call | tf_op jit(solution)/shard_map/coupling/pallas_call | solution.py:498
  59.7 0.6 copy.12
  60.3 0.6 copy.13
  60.9 0.6 %copy.14 = f32[4,3584]{1,0:T(4,128)} copy(f32[4,3584]{1,0:T(4,128)S(1)} %get-tuple-element.5) | data formatting | bytes 114688

commit v6 on v5

--- a/solution.py
+++ b/solution.py
@@ -38,7 +38,7 @@
 def kernel(
     ring, samples, tiles, reach, otiles,
     atm_hbm, owners_hbm, otile_hbm, cent_hbm, w_hbm, ocean_hbm,
-    flux_out, ocean_out, atm_out,
+    out,
     rows_next, rows_back, atm, owners, otile, cent, w, ocean,
     val, part, pick, pick_t, spread, oc, table, col_inverse, lhs,
     send0, recv0, ends_sent, ends_got, send1a, recv1a, send1, recv1, send2a, recv2a, send2, recv2,
@@ -173,29 +173,36 @@
         place = (1 - core) * low + core * high
         return jnp.where(owner < cols, group * slots + rank * ring + place, -1)
 
-    tile_down = jnp.broadcast_to(tile_across, (entries, entries)).T
-
-    def end_rows(x):
-        at = [k * PAD for k in range(reach)] + [k * PAD + tiles - 1 for k in range(reach)]
-        return jnp.concatenate([x[i : i + 1] for i in at], axis=0)
-
-    end_owner = end_rows(owner_down).astype(I32)
-    end_high = end_owner // ring
-    end_low = end_owner - end_high * ring
-    end_group = (1 - core) * end_high + core * end_low
-    end_row = ((1 - core) * end_low + core * end_high) * 8 + end_rows(tile_down).astype(I32)
-
-    slot_across = slot(owner_across, rank_across)
-    slot_down = slot(owner_down[:, :1], rank_down)
+    def place_of(owner):
+        owner = owner.astype(I32)
+        high = owner // ring
+        low = owner - high * ring
+        return (1 - core) * high + core * low, (1 - core) * low + core * high
+
+    group_across, place_across = place_of(owner_across)
+    group_down, place_down = place_of(owner_down)
+    slot_across = jnp.where(owner_across < cols, group_across * slots + rank_across * ring + place_across, -1)
+    seat_down = rank_down * ring + place_down
+    slot_down = jnp.where(owner_down < cols, group_down * slots + seat_down, -1)[:, :1]
     pick_f = (lax.broadcasted_iota(I32, (rows, entries), 0) == slot_across).astype(F32)
     pick[...] = twice(pick_f.astype(BF16))
     pick_b = (lax.broadcasted_iota(I32, (entries, rows), 1) == slot_down).astype(F32).astype(BF16)
     pick_t[...] = twice(pick_b)
-    named = jnp.sum(pick_f * (tile_across + 1.0), axis=1, keepdims=True)
-    named = jnp.broadcast_to(named - 1.0, (rows, TILE))
+
+    stride = slots + ends
+    per_line = TILE // stride
+    base = (first % per_line) * stride
+    ocean_row = place_across * 8 + tile_across.astype(I32) + 1
+    group_row = lax.broadcasted_iota(I32, (8, entries), 0) == group_across
+    marked = jnp.where(group_row & (owner_across < cols), ocean_row, 0).astype(F32).astype(BF16)
+    tile_at, k_at = at_row % PAD, at_row // PAD
+    seated = (at_lane == base + seat_down) & (owner_down < cols)
+    seated = seated | (tile_at == 0) & (at_lane == base + slots + k_at)
+    seated = seated | (tile_at == tiles - 1) & (at_lane == base + slots + reach + k_at)
+    named = jnp.dot(marked, seated.astype(F32).astype(BF16), preferred_element_type=F32)
+    line_of = lax.broadcasted_iota(I32, (8, TILE), 0) == first // per_line
     for g in range(ring):
-        send0[g, :slots] = named[g * slots : (g + 1) * slots]
-        send0[g, slots : slots + ends] = jnp.where(end_group == g, end_row, -1).astype(F32)
+        send0[g, :8] = jnp.where(line_of, named[g : g + 1], 0.0)
     send_named, arrive0, leave0 = exchange(0, ring, first, on_first, lambda p: send0.at[p], recv0)
 
     small[4].wait()
@@ -255,11 +262,11 @@
     high_weights = [x[FIELDS + 2 : FIELDS + 3] for x in tile_sums(tiles - 1, cut)]
     end_weights = jnp.concatenate(low_weights + high_weights, axis=0)
     for g in range(ring):
-        send0[g, slots + ends :] = end_weights
+        send0[g, 8:] = end_weights
     for q in range(rest):
         inner_sums(1 + 4 * groups + q)
 
-    early = min(groups, 3)
+    early = min(groups, 5)
     lax.fori_loop(0, early, group_sums, 0)
     pl.semaphore_wait(barrier, 3 + 2 * (ring - 1) + chips - 1)
     send_named()
@@ -275,9 +282,9 @@
     send()
     sent1 = []
     for m in range(2):
-        codes = []
-        for f in range(4 * m, 4 * m + 4):
-            codes.append(mixed(pick[...], part[f * entries : (f + 1) * entries]))
+        codes = [part[f * entries : (f + 1) * entries] for f in range(4 * m, 4 * m + 4)]
+        codes = mixed(pick[...], jnp.concatenate(codes, axis=1))
+        codes = [codes[:, i * TILE : (i + 1) * TILE] for i in range(4)]
         for g in range(ring):
             block = jnp.concatenate([x[g * slots : (g + 1) * slots] for x in codes], axis=0)
             send1[m, g] = block.astype(I32).astype(I16)
@@ -304,15 +311,19 @@
     ends_got[first] = ends_sent[...]
 
     arrive0()
-    row = lax.broadcasted_iota(I32, (rows, TILE), 0)
-    lane_of = lax.broadcasted_iota(I32, (rows, TILE), 1)
-    target = recv0[:, :slots].reshape(rows, TILE).astype(I32)
-    member = ((target >= 0) & (target + 8 * (row % ring) == lane_of)).astype(F32)
-    spread[...] = twice(member[:, : 8 * ring].astype(BF16))
-    target = recv0[:, slots : slots + ends].reshape(ring * ends, TILE).astype(I32)
-    member_ends = (target == lax.broadcasted_iota(I32, (ring * ends, TILE), 1)).astype(F32)
-    gather = twice(jnp.concatenate([member, member_ends], axis=0).T[: 8 * ring].astype(BF16))
-    end_weights = recv0[:, slots + ends :].reshape(ring * ends, TILE) * LEVELS
+    lines = jnp.zeros((8, TILE), F32)
+    for p in range(ring):
+        lines = lines + recv0[p, :8]
+    want = (lax.broadcasted_iota(I32, (TILE, TILE), 0) + 1).astype(F32)
+    member = [(want == lines[i : i + 1]).astype(F32) for i in range(-(-ring // per_line))]
+    gather = jnp.concatenate(member, axis=1)[: 8 * ring, : ring * stride]
+    gather = twice(gather.astype(BF16))
+    back_rows = jnp.concatenate([x.T for x in member], axis=0)[: ring * stride, : 8 * ring]
+    spread[...] = twice(back_rows.astype(BF16))
+    end_weights = recv0[:, 8:] * LEVELS
+
+    def stacked(of_slots, of_ends):
+        return jnp.concatenate([of_slots, of_ends], axis=1).reshape(ring * stride, TILE)
 
     def column_area(c, carry):
         for q in range(chunk):
@@ -326,15 +337,15 @@
 
     send, arrive2a, leave2a = exchange(5, ring, second, on_second, lambda p: send2a.at[p], recv2a)
     arrive1a()
-    areas = recv1a[...].reshape(rows, TILE)
-    dense_area = mixed(gather, jnp.concatenate([areas, jnp.zeros((ring * ends, TILE), F32)], axis=0))
+    areas = recv1a[...]
+    dense_area = mixed(gather, stacked(areas, jnp.zeros((ring, ends, TILE), F32)))
     send2a[...] = dense_area.reshape(ring, 8, TILE)
     send()
     recv2a[second] = send2a[second]
     per_area = 1.0 / jnp.maximum(dense_area, LEAST)
     send, arrive2, leave2 = exchange(6, ring, second, on_second, lambda p: send2.at[p], recv2)
     arrive_ends()
-    end_values = ends_got[...].reshape(ring * ends, TILE)
+    end_values = ends_got[...]
     for m in range(2):
         arrive, _ = sent1[m]
         arrive()
@@ -342,8 +353,8 @@
         means = []
         for i in range(4):
             f = 4 * m + i
-            sums = block[:, i * slots : (i + 1) * slots].reshape(rows, TILE) * areas
-            sums = jnp.concatenate([sums, end_values[:, f : f + 1] * end_weights], axis=0)
+            sums = block[:, i * slots : (i + 1) * slots] * areas
+            sums = stacked(sums, end_values[:, :, f : f + 1] * end_weights)
             means.append((mixed(gather, sums) * per_area).reshape(ring, 8, TILE))
         block = jnp.concatenate(means, axis=1)
         send2[:, 32 * m : 32 * m + 32] = jnp.round(block).astype(I32).astype(I16)
@@ -391,7 +402,7 @@
     recv3y[chip] = send3y[...]
     for i, flux in enumerate((stress_u, stress_v, net_heat, freshwater)):
         for t in range(otiles):
-            flux_out[0, i : i + 1, t * TILE : (t + 1) * TILE] = flux[t : t + 1]
+            out[i : i + 1, t * TILE : (t + 1) * TILE] = flux[t : t + 1]
     for leave in (leave0, leave1a, leave_ends, leave2a, leave2, to_right.wait_send, to_left.wait_send):
         leave()
     for _, leave in sent1:
@@ -417,14 +428,14 @@
     slotted = mixed(spread[...], jnp.concatenate(states, axis=1))
     for p in range(ring):
         for r in range(2):
-            send5[p, r] = slotted[p * slots : (p + 1) * slots, r * TILE : (r + 1) * TILE]
+            send5[p, r] = slotted[p * stride : p * stride + slots, r * TILE : (r + 1) * TILE]
     send, arrive, leave5 = exchange(9, ring, first, on_first, lambda p: send5.at[p], recv5)
     send()
     recv5[first] = send5[first]
     to_sibling(1, rows_next.at[mine], rows_next.at[other]).wait_recv()
     for r in range(4):
         for t in range(otiles):
-            ocean_out[r : r + 1, t * TILE : (t + 1) * TILE] = rows_next[r, t : t + 1]
+            out[r : r + 1, (otiles + t) * TILE : (otiles + t + 1) * TILE] = rows_next[r, t : t + 1]
     ocean_copy.wait_send()
     leave4()
     arrive()
@@ -471,7 +482,7 @@
         to_sibling(2 + j, rows_back.at[mine, at], rows_back.at[other, at]).wait_recv()
         for r in range(4):
             for t in range(8 * j, min(8 * j + 8, tiles)):
-                atm_out[r : r + 1, t * TILE : (t + 1) * TILE] = rows_back[r, t : t + 1]
+                out[r : r + 1, (2 * otiles + t) * TILE : (2 * otiles + t + 1) * TILE] = rows_back[r, t : t + 1]
     for j in range(whole + (last > 0)):
         results(j).wait_send()
 
@@ -490,16 +501,11 @@
     entries = reach * PAD
     hbm = pl.BlockSpec(memory_space=pltpu.HBM)
     vmem = pl.BlockSpec(memory_space=pltpu.VMEM)
-    out_shape = (
-        jax.ShapeDtypeStruct((1, 4, ocells), F32),
-        jax.ShapeDtypeStruct((4, ocells), F32),
-        jax.ShapeDtypeStruct((4, cells), F32),
-    )
     results = pl.pallas_call(
         functools.partial(kernel, ring, samples, tiles, reach, otiles),
-        out_shape=tuple(pltpu.VMEM(s.shape, s.dtype) for s in out_shape),
+        out_shape=pltpu.VMEM((4, 2 * ocells + cells), F32),
         in_specs=[hbm] * 6,
-        out_specs=(vmem, vmem, vmem),
+        out_specs=vmem,
         scratch_shapes=[
             pltpu.VMEM((4, 8, TILE), F32),
             pltpu.VMEM((4, PAD, TILE), F32),
@@ -513,13 +519,13 @@
             pltpu.VMEM(((FIELDS + 1) * entries, TILE), F32),
             pltpu.VMEM((rows, 2 * entries), BF16),
             pltpu.VMEM((entries, 2 * rows), BF16),
-            pltpu.VMEM((rows, 16 * ring), BF16),
+            pltpu.VMEM((ring * (slots + 2 * reach), 16 * ring), BF16),
             pltpu.VMEM((4, 8, TILE), F32),
             pltpu.VMEM((8, TILE), F32),
             pltpu.VMEM((PAD, TILE), F32),
             pltpu.VMEM((PAD // 8, 32, reach * TILE), BF16),
-            pltpu.VMEM((ring, slots + 4 * reach, TILE), F32),
-            pltpu.VMEM((ring, slots + 4 * reach, TILE), F32),
+            pltpu.VMEM((ring, 8 + 2 * reach, TILE), F32),
+            pltpu.VMEM((ring, 8 + 2 * reach, TILE), F32),
             pltpu.VMEM((2 * reach, TILE), F32),
             pltpu.VMEM((ring, 2 * reach, TILE), F32),
             pltpu.VMEM((ring, slots, TILE), F32),
@@ -552,7 +558,7 @@
         ),
         name="coupling",
     )(atm_state, owners.T, ocean_tile.T, centroid_offset, remap_weight, ocean_state)
-    return results
+    return results[None, :, :ocells], results[:, ocells : 2 * ocells], results[:, 2 * ocells :]
 
 
 def solution(mesh):

time: 61.6 us -> 60.2 us (0.977)
  Pallas kernels: 59 us -> 58.1 us
    unnamed x3 -> x0, local copies, waits for them, and re-layouts: 1.82 us -> none
    slice x0 -> x2, local copies, waits for them, and re-layouts: none -> 1.24 us  [the longest x1 0.63 us: shards(): results[:, 2 * ocells:]]
    pallas_call x1, Pallas kernels: 59 us -> 58.1 us  [shards(): pl.pallas_call(functools.partial(kernel, ring, samples, tiles, reach, oti...]
where the time goes in v6:
time: 60.2 us; the launch traced here: 60 us
  Pallas kernels  58.1 us (97%)
  local copies, waits for them, and re-layouts  1.24 us (2%)
  between operations  0.64 us (1%)
    pallas_call x1, Pallas kernels, shards(): pl.pallas_call(functools.partial(kernel, ring, samples, tiles, reach, oti...  58.1 us

profile of v6, /device:TPU:1, one launch (start us, length us, event | category | flops | bytes accessed | tf_op | source)
XLA Modules:
  0.0 60.0 jit_solution(4454057355246075266)
XLA Ops:
  0.6 58.1 %coupling.1 = f32[4,5376]{1,0:T(4,128)S(1)} custom-call(bf16[1,8,3584]{2,1,0:T(8,128)(2,1)} %atm_hbm.1, s32[4,28]{1,0:T(4,128)} %bitcast.4, s32[4,28]{1,0:T(4,128)} %bitcast.5, f32[28,4,128]{2,1,0:T(4,128)} %cent_hbm.1, bf16[28,4,128,128]{3,2,1,0:T(8,128)(2,1)} %w_hbm.1, f32[4,896]{1,0:T(4,128)} %ocean_hbm.1), custom_call_target="tpu_custom_call" | custom-call | tf_op jit(solution)/shard_map/coupling/pallas_call | solution.py:504
  58.8 0.6 %fusion = (f32[4,896]{1,0:T(4,128)}, f32[1,4,896]{2,1,0:T(4,128)}) fusion(f32[4,5376]{1,0:T(4,128)S(1)} %coupling.1), kind=kLoop, calls=%fused_computation.1 | loop fusion | bytes 57344 | tf_op jit(solution)/shard_map/slice | solution.py:561
  59.4 0.6 %slice.11 = f32[4,3584]{1,0:T(4,128)} slice(f32[4,5376]{1,0:T(4,128)S(1)} %coupling.1), slice={[0:4], [1792:5376]} | slice | bytes 114688 | tf_op jit(solution)/shard_map/slice | solution.py:561

commit v7 on v6

--- a/solution.py
+++ b/solution.py
@@ -343,50 +343,57 @@
     send()
     recv2a[second] = send2a[second]
     per_area = 1.0 / jnp.maximum(dense_area, LEAST)
-    send, arrive2, leave2 = exchange(6, ring, second, on_second, lambda p: send2.at[p], recv2)
     arrive_ends()
     end_values = ends_got[...]
+    sent2 = []
     for m in range(2):
         arrive, _ = sent1[m]
         arrive()
         block = recv1[m].astype(I32).astype(F32)
-        means = []
+        sums = []
         for i in range(4):
             f = 4 * m + i
-            sums = block[:, i * slots : (i + 1) * slots] * areas
-            sums = stacked(sums, end_values[:, :, f : f + 1] * end_weights)
-            means.append((mixed(gather, sums) * per_area).reshape(ring, 8, TILE))
-        block = jnp.concatenate(means, axis=1)
-        send2[:, 32 * m : 32 * m + 32] = jnp.round(block).astype(I32).astype(I16)
-    send()
-    recv2[second] = send2[second]
+            field = block[:, i * slots : (i + 1) * slots] * areas
+            sums.append(stacked(field, end_values[:, :, f : f + 1] * end_weights))
+        dense = mixed(gather, jnp.concatenate(sums, axis=1))
+        means = [(dense[:, i * TILE : (i + 1) * TILE] * per_area).reshape(ring, 8, TILE) for i in range(4)]
+        send2[m] = jnp.round(jnp.concatenate(means, axis=1)).astype(I32).astype(I16)
+        send, *done = exchange(6 + m, ring, second, on_second, lambda p: send2.at[m, p], recv2.at[m])
+        send()
+        sent2.append(done)
+        recv2[m, second] = send2[m, second]
     arrive2a()
-    arrive2()
 
     coverage = jnp.zeros((8, TILE), F32)
-    total = jnp.zeros((FIELDS, 8, TILE), F32)
     for p in range(ring):
-        area = recv2a[p]
-        coverage = coverage + area
-        total = total + recv2[p].astype(I32).astype(F32).reshape(FIELDS, 8, TILE) * area[None]
-    forcing = total * (1.0 / (LEVELS * jnp.maximum(coverage, 1.0)))[None]
-
-    sst, uo, vo = oc[0], oc[1], oc[2]
-    slip_u = forcing[0] - uo
-    slip_v = forcing[1] - vo
-    wind_speed = jnp.sqrt(slip_u * slip_u + slip_v * slip_v + 0.25)
-    saturation = 0.9 * jnp.exp(0.07 * sst - 0.1 * forcing[4])
-    sensible = 0.4 * wind_speed * (sst - forcing[2])
-    latent = 0.4 * wind_speed * (saturation - forcing[3])
+        coverage = coverage + recv2a[p]
+    per_coverage = 1.0 / (LEVELS * jnp.maximum(coverage, 1.0))
+
+    def half_forcing(m):
+        arrive, _ = sent2[m]
+        arrive()
+        total = jnp.zeros((4, 8, TILE), F32)
+        for p in range(ring):
+            total = total + recv2[m, p].astype(I32).astype(F32).reshape(4, 8, TILE) * recv2a[p][None]
+        return total * per_coverage[None]
 
     def softplus(v):
         return jnp.maximum(v, 0.0) + jnp.log1p(jnp.exp(-jnp.abs(v)))
 
+    sst, uo, vo = oc[0], oc[1], oc[2]
     insolation = 0.5 + 1.5 * fld.astype(F32) / (samples - 1)
-    net_heat = insolation * softplus(forcing[5]) + 0.3 * forcing[6] - 0.1 * sst - sensible - latent
-    freshwater = softplus(forcing[7]) - latent
+    wind_u, wind_v, air, vapour = half_forcing(0)
+    slip_u = wind_u - uo
+    slip_v = wind_v - vo
+    wind_speed = jnp.sqrt(slip_u * slip_u + slip_v * slip_v + 0.25)
+    sensible = 0.4 * wind_speed * (sst - air)
     stress_u = 0.5 * wind_speed * slip_u
     stress_v = 0.5 * wind_speed * slip_v
+    pressure, short, long, rain = half_forcing(1)
+    saturation = 0.9 * jnp.exp(0.07 * sst - 0.1 * pressure)
+    latent = 0.4 * wind_speed * (saturation - vapour)
+    net_heat = insolation * softplus(short) + 0.3 * long - 0.1 * sst - sensible - latent
+    freshwater = softplus(rain) - latent
     send3[0] = net_heat
     send3[1] = stress_u
     send3[2] = stress_v
@@ -397,15 +404,15 @@
     pair_copy.start()
     pair_copy.wait_recv()
     send3y[...] = send3[mine] + recv3[...]
-    send, arrive, leave3 = exchange(7, chips, chip, on_chip, lambda p: send3y, recv3y)
+    send, arrive, leave3 = exchange(8, chips, chip, on_chip, lambda p: send3y, recv3y)
     send()
     recv3y[chip] = send3y[...]
     for i, flux in enumerate((stress_u, stress_v, net_heat, freshwater)):
         for t in range(otiles):
             out[i : i + 1, t * TILE : (t + 1) * TILE] = flux[t : t + 1]
-    for leave in (leave0, leave1a, leave_ends, leave2a, leave2, to_right.wait_send, to_left.wait_send):
+    for leave in (leave0, leave1a, leave_ends, leave2a, to_right.wait_send, to_left.wait_send):
         leave()
-    for _, leave in sent1:
+    for _, leave in sent1 + sent2:
         leave()
     pair_copy.wait_send()
     arrive()
@@ -415,7 +422,7 @@
     state = oc[mine] + (0.5 / samples) * flux_sum
     send4[...] = state
 
-    send, arrive, leave4 = exchange(8, ring, second, on_second, lambda p: send4, recv4)
+    send, arrive, leave4 = exchange(9, ring, second, on_second, lambda p: send4, recv4)
     send()
     recv4[second] = state
     rows_next[mine] = state
@@ -429,7 +436,7 @@
     for p in range(ring):
         for r in range(2):
             send5[p, r] = slotted[p * stride : p * stride + slots, r * TILE : (r + 1) * TILE]
-    send, arrive, leave5 = exchange(9, ring, first, on_first, lambda p: send5.at[p], recv5)
+    send, arrive, leave5 = exchange(10, ring, first, on_first, lambda p: send5.at[p], recv5)
     send()
     recv5[first] = send5[first]
     to_sibling(1, rows_next.at[mine], rows_next.at[other]).wait_recv()
@@ -534,8 +541,8 @@
             pltpu.VMEM((2, ring, 4 * slots, TILE), I16),
             pltpu.VMEM((ring, 8, TILE), F32),
             pltpu.VMEM((ring, 8, TILE), F32),
-            pltpu.VMEM((ring, FIELDS * 8, TILE), I16),
-            pltpu.VMEM((ring, FIELDS * 8, TILE), I16),
+            pltpu.VMEM((2, ring, 4 * 8, TILE), I16),
+            pltpu.VMEM((2, ring, 4 * 8, TILE), I16),
             pltpu.VMEM((4, 8, TILE), F32),
             pltpu.VMEM((2, 8, TILE), F32),
             pltpu.VMEM((2, 8, TILE), F32),
@@ -548,8 +555,8 @@
             pltpu.SemaphoreType.DMA((tiles,)),
             pltpu.SemaphoreType.DMA((2,)),
             pltpu.SemaphoreType.DMA((2,)),
-            pltpu.SemaphoreType.DMA((10,)),
-            pltpu.SemaphoreType.DMA((10,)),
+            pltpu.SemaphoreType.DMA((11,)),
+            pltpu.SemaphoreType.DMA((11,)),
             pltpu.SemaphoreType.DMA((2 + PAD // 8,)),
             pltpu.SemaphoreType.DMA((2 + PAD // 8,)),
         ],

time: 60.2 us -> 60.1 us (level)
  no operation moved by 1% of the time
where the time goes in v7:
time: 60.1 us; the launch traced here: 60 us
  Pallas kernels  58.1 us (97%)
  local copies, waits for them, and re-layouts  1.24 us (2%)
  between operations  0.64 us (1%)
    pallas_call x1, Pallas kernels, shards(): pl.pallas_call(functools.partial(kernel, ring, samples, tiles, reach, oti...  58.1 us

profile of v7, /device:TPU:1, one launch (start us, length us, event | category | flops | bytes accessed | tf_op | source)
XLA Modules:
  0.0 60.0 jit_solution(8018949118966986028)
XLA Ops:
  0.6 58.1 %coupling.1 = f32[4,5376]{1,0:T(4,128)S(1)} custom-call(bf16[1,8,3584]{2,1,0:T(8,128)(2,1)} %atm_hbm.1, s32[4,28]{1,0:T(4,128)} %bitcast.4, s32[4,28]{1,0:T(4,128)} %bitcast.5, f32[28,4,128]{2,1,0:T(4,128)} %cent_hbm.1, bf16[28,4,128,128]{3,2,1,0:T(8,128)(2,1)} %w_hbm.1, f32[4,896]{1,0:T(4,128)} %ocean_hbm.1), custom_call_target="tpu_custom_call" | custom-call | tf_op jit(solution)/shard_map/coupling/pallas_call | solution.py:511
  58.7 0.6 %fusion = (f32[4,896]{1,0:T(4,128)}, f32[1,4,896]{2,1,0:T(4,128)}) fusion(f32[4,5376]{1,0:T(4,128)S(1)} %coupling.1), kind=kLoop, calls=%fused_computation.1 | loop fusion | bytes 57344 | tf_op jit(solution)/shard_map/slice | solution.py:568
  59.3 0.6 %slice.11 = f32[4,3584]{1,0:T(4,128)} slice(f32[4,5376]{1,0:T(4,128)S(1)} %coupling.1), slice={[0:4], [1792:5376]} | slice | bytes 114688 | tf_op jit(solution)/shard_map/slice | solution.py:568

commit v8 on v7

--- a/solution.py
+++ b/solution.py
@@ -14,6 +14,9 @@
 PAD = 32
 LEVELS = 5400.0
 LEAST = 1e-30
+SMALLEST = 2.0**-24
+STEP = 31.0 * math.log(2.0) / 65534.0
+MIDDLE = -8.5 * math.log(2.0)
 MESH = pl.DeviceIdType.MESH
 F32 = jnp.float32
 BF16 = jnp.bfloat16
@@ -78,14 +81,16 @@
     def far_first(count):
         return sorted(range(1, count), key=lambda d: -min(d, count - d))
 
-    for d in far_first(ring):
-        greet(on_first((first + d) % ring))
-        greet(on_second((second + d) % ring))
-    for d in far_first(chips):
-        greet(on_chip((chip + d) % chips))
-    greet((left, fld))
-    greet((right, fld))
-    greet(sibling)
+    def greet_all(far):
+        for d in far_first(ring):
+            if (min(d, ring - d) >= 3) == far:
+                greet(on_first((first + d) % ring))
+                greet(on_second((second + d) % ring))
+        for d in far_first(chips):
+            if (min(d, chips - d) >= 3) == far:
+                greet(on_chip((chip + d) % chips))
+
+    greet_all(True)
 
     small = [
         pltpu.make_async_copy(source, target, in_sem.at[i])
@@ -104,6 +109,11 @@
 
     for c in (groups + 1, groups, *range(groups)):
         weights(c).start()
+
+    greet_all(False)
+    greet((left, fld))
+    greet((right, fld))
+    greet(sibling)
 
     def exchange(stage, count, me, device, source, target):
         def send():
@@ -237,10 +247,8 @@
         )
         for k in range(reach):
             sums = product[16 * k : 16 * k + 16, k // 2 * TILE : (k // 2 + 1) * TILE]
-            area = sums[FIELDS : FIELDS + 1]
-            code = jnp.round(sums[:FIELDS] * (LEVELS / jnp.maximum(area, LEAST)))
-            part[pl.ds(k * PAD + t, FIELDS, stride=entries), :] = code
-            part[pl.ds(FIELDS * entries + k * PAD + t, 1), :] = area
+            part[pl.ds(k * PAD + t, FIELDS, stride=entries), :] = sums[:FIELDS]
+            part[pl.ds(FIELDS * entries + k * PAD + t, 1), :] = sums[FIELDS : FIELDS + 1]
         return [product[16 * k : 16 * k + 16, k // 2 * TILE : (k // 2 + 1) * TILE] for k in range(reach)]
 
     def inner_sums(t):
@@ -275,25 +283,28 @@
     recv0[first] = send0[first]
     lax.fori_loop(early, groups, group_sums, 0)
 
-    send, arrive1a, leave1a = exchange(1, ring, first, on_first, lambda p: send1a.at[p], recv1a)
-    slotted = mixed(pick[...], part[FIELDS * entries :])
-    for g in range(ring):
-        send1a[g] = slotted[g * slots : (g + 1) * slots]
-    send()
+    area_code = jnp.maximum(part[FIELDS * entries :], SMALLEST)
+    area_code = jnp.round((jnp.log(area_code) - MIDDLE) * (1.0 / STEP))
+    area_code = jnp.clip(area_code, -32767.0, 32767.0)
+    scale = LEVELS / jnp.exp(area_code * STEP + MIDDLE)
     sent1 = []
-    for m in range(2):
-        codes = [part[f * entries : (f + 1) * entries] for f in range(4 * m, 4 * m + 4)]
+    for m, (source, target) in enumerate(((send1a, recv1a), (send1, recv1))):
+        codes = [jnp.round(part[f * entries : (f + 1) * entries] * scale) for f in range(4 * m, 4 * m + 4)]
+        if m == 0:
+            codes.append(area_code)
+        count = len(codes)
         codes = mixed(pick[...], jnp.concatenate(codes, axis=1))
-        codes = [codes[:, i * TILE : (i + 1) * TILE] for i in range(4)]
+        codes = [codes[:, i * TILE : (i + 1) * TILE] for i in range(count)]
         for g in range(ring):
-            block = jnp.concatenate([x[g * slots : (g + 1) * slots] for x in codes], axis=0)
-            send1[m, g] = block.astype(I32).astype(I16)
-        send, *done = exchange(2 + m, ring, first, on_first, lambda p: send1.at[m, p], recv1.at[m])
+            block = [x[g * slots : (g + 1) * slots] for x in codes]
+            if source.shape[1] > count * slots:
+                block.append(jnp.zeros((source.shape[1] - count * slots, TILE), F32))
+            source[g] = jnp.concatenate(block, axis=0).astype(I32).astype(I16)
+        send, *done = exchange(1 + m, ring, first, on_first, lambda p: source.at[p], target)
         send()
         sent1.append(done)
     recv1a[first] = send1a[first]
-    for m in range(2):
-        recv1[m, first] = send1[m, first]
+    recv1[first] = send1[first]
 
     to_right.wait_recv()
     to_left.wait_recv()
@@ -336,8 +347,9 @@
     lax.fori_loop(0, tiles // chunk, column_area, 0)
 
     send, arrive2a, leave2a = exchange(5, ring, second, on_second, lambda p: send2a.at[p], recv2a)
-    arrive1a()
-    areas = recv1a[...]
+    sent1[0][0]()
+    codes1 = recv1a[...].astype(I32).astype(F32)
+    areas = jnp.exp(codes1[:, 4 * slots : 5 * slots] * STEP + MIDDLE)
     dense_area = mixed(gather, stacked(areas, jnp.zeros((ring, ends, TILE), F32)))
     send2a[...] = dense_area.reshape(ring, 8, TILE)
     send()
@@ -347,13 +359,13 @@
     end_values = ends_got[...]
     sent2 = []
     for m in range(2):
-        arrive, _ = sent1[m]
-        arrive()
-        block = recv1[m].astype(I32).astype(F32)
+        if m == 1:
+            sent1[1][0]()
+            codes1 = recv1[...].astype(I32).astype(F32)
         sums = []
         for i in range(4):
             f = 4 * m + i
-            field = block[:, i * slots : (i + 1) * slots] * areas
+            field = codes1[:, i * slots : (i + 1) * slots] * areas
             sums.append(stacked(field, end_values[:, :, f : f + 1] * end_weights))
         dense = mixed(gather, jnp.concatenate(sums, axis=1))
         means = [(dense[:, i * TILE : (i + 1) * TILE] * per_area).reshape(ring, 8, TILE) for i in range(4)]
@@ -410,7 +422,7 @@
     for i, flux in enumerate((stress_u, stress_v, net_heat, freshwater)):
         for t in range(otiles):
             out[i : i + 1, t * TILE : (t + 1) * TILE] = flux[t : t + 1]
-    for leave in (leave0, leave1a, leave_ends, leave2a, to_right.wait_send, to_left.wait_send):
+    for leave in (leave0, leave_ends, leave2a, to_right.wait_send, to_left.wait_send):
         leave()
     for _, leave in sent1 + sent2:
         leave()
@@ -535,10 +547,10 @@
             pltpu.VMEM((ring, 8 + 2 * reach, TILE), F32),
             pltpu.VMEM((2 * reach, TILE), F32),
             pltpu.VMEM((ring, 2 * reach, TILE), F32),
-            pltpu.VMEM((ring, slots, TILE), F32),
-            pltpu.VMEM((ring, slots, TILE), F32),
-            pltpu.VMEM((2, ring, 4 * slots, TILE), I16),
-            pltpu.VMEM((2, ring, 4 * slots, TILE), I16),
+            pltpu.VMEM((ring, -(-5 * slots // 16) * 16, TILE), I16),
+            pltpu.VMEM((ring, -(-5 * slots // 16) * 16, TILE), I16),
+            pltpu.VMEM((ring, 4 * slots, TILE), I16),
+            pltpu.VMEM((ring, 4 * slots, TILE), I16),
             pltpu.VMEM((ring, 8, TILE), F32),
             pltpu.VMEM((ring, 8, TILE), F32),
             pltpu.VMEM((2, ring, 4 * 8, TILE), I16),

time: 60.1 us -> 59.6 us (level)
  no operation moved by 1% of the time
where the time goes in v8:
time: 59.6 us; the launch traced here: 59.4 us
  Pallas kernels  57.6 us (97%)
  local copies, waits for them, and re-layouts  1.24 us (2%)
  between operations  0.64 us (1%)
    pallas_call x1, Pallas kernels, shards(): pl.pallas_call(functools.partial(kernel, ring, samples, tiles, reach, oti...  57.6 us

profile of v8, /device:TPU:1, one launch (start us, length us, event | category | flops | bytes accessed | tf_op | source)
XLA Modules:
  0.0 59.4 jit_solution(9350900113538739141)
XLA Ops:
  0.6 57.6 %coupling.1 = f32[4,5376]{1,0:T(4,128)S(1)} custom-call(bf16[1,8,3584]{2,1,0:T(8,128)(2,1)} %atm_hbm.1, s32[4,28]{1,0:T(4,128)} %bitcast.4, s32[4,28]{1,0:T(4,128)} %bitcast.5, f32[28,4,128]{2,1,0:T(4,128)} %cent_hbm.1, bf16[28,4,128,128]{3,2,1,0:T(8,128)(2,1)} %w_hbm.1, f32[4,896]{1,0:T(4,128)} %ocean_hbm.1), custom_call_target="tpu_custom_call" | custom-call | tf_op jit(solution)/shard_map/coupling/pallas_call | solution.py:523
  58.2 0.6 %fusion = (f32[4,896]{1,0:T(4,128)}, f32[1,4,896]{2,1,0:T(4,128)}) fusion(f32[4,5376]{1,0:T(4,128)S(1)} %coupling.1), kind=kLoop, calls=%fused_computation.1 | loop fusion | bytes 57344 | tf_op jit(solution)/shard_map/slice | solution.py:580
  58.8 0.6 %slice.11 = f32[4,3584]{1,0:T(4,128)} slice(f32[4,5376]{1,0:T(4,128)S(1)} %coupling.1), slice={[0:4], [1792:5376]} | slice | bytes 114688 | tf_op jit(solution)/shard_map/slice | solution.py:580

commit v9 on v8

--- a/solution.py
+++ b/solution.py
@@ -329,8 +329,12 @@
     member = [(want == lines[i : i + 1]).astype(F32) for i in range(-(-ring // per_line))]
     gather = jnp.concatenate(member, axis=1)[: 8 * ring, : ring * stride]
     gather = twice(gather.astype(BF16))
-    back_rows = jnp.concatenate([x.T for x in member], axis=0)[: ring * stride, : 8 * ring]
-    spread[...] = twice(back_rows.astype(BF16))
+    back_rows = jnp.concatenate([x.T for x in member], axis=0)[: ring * stride]
+    spread[...] = twice(back_rows[:, : 8 * ring].astype(BF16))
+    end_rows_back = back_rows.reshape(ring, stride, TILE)[:, slots:].reshape(ring * ends, TILE)
+    end_rows_back = [end_rows_back, jnp.zeros((TILE - ring * ends, TILE), F32)]
+    gather_ends = jnp.concatenate(end_rows_back, axis=0).T[: 8 * ring, : ring * ends]
+    gather_ends = twice(gather_ends.astype(BF16))
     end_weights = recv0[:, 8:] * LEVELS
 
     def stacked(of_slots, of_ends):
@@ -355,20 +359,24 @@
     send()
     recv2a[second] = send2a[second]
     per_area = 1.0 / jnp.maximum(dense_area, LEAST)
+    no_ends = jnp.zeros((ring, ends, TILE), F32)
+
+    def dense_sums(codes):
+        sums = [stacked(codes[:, i * slots : (i + 1) * slots] * areas, no_ends) for i in range(4)]
+        return mixed(gather, jnp.concatenate(sums, axis=1))
+
+    def dense_ends(m):
+        sums = [ends_got[:, :, f : f + 1] * end_weights for f in range(4 * m, 4 * m + 4)]
+        return mixed(gather_ends, jnp.concatenate([x.reshape(ring * ends, TILE) for x in sums], axis=1))
+
+    dense = [dense_sums(codes1)]
+    sent1[1][0]()
+    dense.append(dense_sums(recv1[...].astype(I32).astype(F32)))
     arrive_ends()
-    end_values = ends_got[...]
     sent2 = []
     for m in range(2):
-        if m == 1:
-            sent1[1][0]()
-            codes1 = recv1[...].astype(I32).astype(F32)
-        sums = []
-        for i in range(4):
-            f = 4 * m + i
-            field = codes1[:, i * slots : (i + 1) * slots] * areas
-            sums.append(stacked(field, end_values[:, :, f : f + 1] * end_weights))
-        dense = mixed(gather, jnp.concatenate(sums, axis=1))
-        means = [(dense[:, i * TILE : (i + 1) * TILE] * per_area).reshape(ring, 8, TILE) for i in range(4)]
+        total = dense[m] + dense_ends(m)
+        means = [(total[:, i * TILE : (i + 1) * TILE] * per_area).reshape(ring, 8, TILE) for i in range(4)]
         send2[m] = jnp.round(jnp.concatenate(means, axis=1)).astype(I32).astype(I16)
         send, *done = exchange(6 + m, ring, second, on_second, lambda p: send2.at[m, p], recv2.at[m])
         send()

time: 59.6 us -> 59.7 us (level)
  no operation moved by 1% of the time
where the time goes in v9:
time: 59.7 us; the launch traced here: 59.5 us
  Pallas kernels  57.7 us (97%)
  local copies, waits for them, and re-layouts  1.24 us (2%)
  between operations  0.64 us (1%)
    pallas_call x1, Pallas kernels, shards(): pl.pallas_call(functools.partial(kernel, ring, samples, tiles, reach, oti...  57.7 us

profile of v9, /device:TPU:1, one launch (start us, length us, event | category | flops | bytes accessed | tf_op | source)
XLA Modules:
  0.0 59.5 jit_solution(17031339932889868082)
XLA Ops:
  0.6 57.7 %coupling.1 = f32[4,5376]{1,0:T(4,128)S(1)} custom-call(bf16[1,8,3584]{2,1,0:T(8,128)(2,1)} %atm_hbm.1, s32[4,28]{1,0:T(4,128)} %bitcast.4, s32[4,28]{1,0:T(4,128)} %bitcast.5, f32[28,4,128]{2,1,0:T(4,128)} %cent_hbm.1, bf16[28,4,128,128]{3,2,1,0:T(8,128)(2,1)} %w_hbm.1, f32[4,896]{1,0:T(4,128)} %ocean_hbm.1), custom_call_target="tpu_custom_call" | custom-call | tf_op jit(solution)/shard_map/coupling/pallas_call | solution.py:531
  58.3 0.6 %fusion = (f32[4,896]{1,0:T(4,128)}, f32[1,4,896]{2,1,0:T(4,128)}) fusion(f32[4,5376]{1,0:T(4,128)S(1)} %coupling.1), kind=kLoop, calls=%fused_computation.1 | loop fusion | bytes 57344 | tf_op jit(solution)/shard_map/slice | solution.py:588
  58.9 0.6 %slice.11 = f32[4,3584]{1,0:T(4,128)} slice(f32[4,5376]{1,0:T(4,128)S(1)} %coupling.1), slice={[0:4], [1792:5376]} | slice | bytes 114688 | tf_op jit(solution)/shard_map/slice | solution.py:588
